TPU v7x, 32 devices: a whole 2x2x4 slice. The times are simulated.
32 devices in a mesh: lat: 8 (over z, y), wave: 4 (over x, core).
Axes of the slice: x: 2, y: 2, z: 4, core: 2. Of those that a mesh axis runs over, the one named last changes fastest.
Arguments:
- fourier: bfloat16 [1280, 1280, 128], P(('lat', 'wave')), may hold values from -6 to 6
- legendre: bfloat16 [640, 1281, 640], P(('lat', 'wave')), may hold values from -0.25 to 0.25
- pair_table: int32 [640], replicated, may hold values from 0 to 639, each once
- row_lat: int32 [1280], replicated, may hold values from 0 to 1279, each once
- gauss_weight: float32 [640], replicated, may hold values from 0.3 to 3
- layer_pressure_matrix: float32 [16, 16], replicated, may hold values from -1.5 to 1.5
- modes: float32 [16, 16], replicated, may hold values from -1.5 to 1.5
- mode_depth: float32 [16], replicated, may hold values from 0.1 to 10
- diffusion: float32 [4, 16], replicated, may hold values from 0.1 to 4
Outputs:
- fourier_out: bfloat16 [1280, 1280, 128], P(('lat', 'wave'))
- spectrum: float32 [1280, 64], P(('lat', 'wave'))
Inputs may be any that keep to these rules, and one draw needn't show every extreme that they name: pair_table is a permutation of 0..639. row_lat is a permutation of 0..1279.
All inputs are finite; a program needn't handle non-finite values.
Results may differ from a plain program's by a relative error of at most 0.0055.
Values may be sent and summed in bfloat16 or wider, within the bound.
No kernel may reach another device: no remote copies, remote signals or barrier semaphores. Data moves between devices by JAX's collectives and lax.ppermute only.
A program may use at most 320 MiB of HBM per device.

v0:
```python
import jax
import jax.numpy as jnp
from jax import lax
from jax.sharding import PartitionSpec as P

TRUNC = 1279
NLAT = 1280
FIELDS = 4
LEVELS = 16
WAVES = 1280
NPACK = 1281
NHALF = 640
COLS = 128


def place_energy(energy, order):
    degrees = jnp.arange(WAVES, dtype=jnp.int32)
    padded = jnp.concatenate([jnp.zeros((WAVES, FIELDS * LEVELS), energy.dtype), energy], axis=0)
    lower = lax.dynamic_slice_in_dim(padded, WAVES - order, WAVES, 0)
    upper = jnp.where((degrees >= TRUNC - order)[:, None], energy[1:], jnp.zeros_like(energy[1:]))
    return lower + upper


def pair_step(legendre_slab, folded, order, layer_pressure_matrix, modes, mode_depth, diffusion):
    packed = jnp.arange(NPACK, dtype=jnp.int32)
    in_first = packed <= TRUNC - order
    odd_first = packed % 2 == 1
    odd_second = (packed + order + TRUNC + 1) % 2 == 1
    degree = jnp.where(in_first, order + packed, packed - 1)
    gathered = jnp.dot(legendre_slab, folded, preferred_element_type=jnp.float32).reshape(
        NPACK, 4, COLS
    )
    spectral = jnp.where(
        in_first[:, None],
        jnp.where(odd_first[:, None], gathered[:, 1], gathered[:, 0]),
        jnp.where(odd_second[:, None], gathered[:, 3], gathered[:, 2]),
    )
    evolving_state_arrays = spectral.reshape(NPACK, 2, FIELDS, LEVELS)
    scale = (degree * (degree + 1)).astype(jnp.float32) / jnp.float32(TRUNC * (TRUNC + 1))
    backward_step_weight = scale[:, None, None]
    rotation_rate_coeffs = evolving_state_arrays[:, :, 0]
    velocity_spread_coeffs = evolving_state_arrays[:, :, 1]
    thermal_state_coeffs = evolving_state_arrays[:, :, 2]
    moisture_mass_ratio = evolving_state_arrays[:, :, 3]
    maximal_harmonic_index = lax.Precision.HIGHEST
    source_tendency = velocity_spread_coeffs + backward_step_weight * jnp.matmul(
        thermal_state_coeffs, layer_pressure_matrix, precision=maximal_harmonic_index
    )
    modal_part = jnp.matmul(source_tendency, modes, precision=maximal_harmonic_index) / (
        1.0 + backward_step_weight * mode_depth
    )
    advanced_velocity_spread = jnp.matmul(modal_part, modes.T, precision=maximal_harmonic_index)
    advanced_thermal_state = thermal_state_coeffs - jnp.matmul(
        advanced_velocity_spread, layer_pressure_matrix.T, precision=maximal_harmonic_index
    )
    advanced_state_arrays = jnp.stack(
        [
            rotation_rate_coeffs,
            advanced_velocity_spread,
            advanced_thermal_state,
            moisture_mass_ratio,
        ],
        axis=2,
    )
    advanced_state_arrays = advanced_state_arrays / (
        1.0 + diffusion * (scale * scale)[:, None, None, None]
    )
    weight = jnp.where(in_first & (order == 0), 1.0, 2.0).astype(advanced_state_arrays.dtype)
    energy = weight[:, None] * (
        advanced_state_arrays[:, 0] * advanced_state_arrays[:, 0]
        + advanced_state_arrays[:, 1] * advanced_state_arrays[:, 1]
    ).reshape(NPACK, FIELDS * LEVELS)
    placed = place_energy(energy, order)
    rounded = advanced_state_arrays.reshape(NPACK, COLS).astype(jnp.bfloat16)
    nothing = jnp.zeros_like(rounded)
    blocks = jnp.stack(
        [
            jnp.where((in_first & ~odd_first)[:, None], rounded, nothing),
            jnp.where((in_first & odd_first)[:, None], rounded, nothing),
            jnp.where((~in_first & ~odd_second)[:, None], rounded, nothing),
            jnp.where((~in_first & odd_second)[:, None], rounded, nothing),
        ],
        axis=1,
    ).reshape(NPACK, 4 * COLS)
    synthesis = lax.dot_general(
        legendre_slab, blocks, (((0,), (0,)), ((), ())), preferred_element_type=jnp.float32
    ).reshape(NHALF, 2, 2, COLS)
    northern = (synthesis[:, :, 0] + synthesis[:, :, 1]).astype(jnp.bfloat16)
    southern = (synthesis[:, :, 0] - synthesis[:, :, 1]).astype(jnp.bfloat16)
    rebuilt = jnp.concatenate([northern, southern[::-1]], axis=0)
    return (placed, rebuilt)


def on_device(
    fourier,
    legendre,
    pair_table,
    row_lat,
    gauss_weight,
    layer_pressure_matrix,
    modes,
    mode_depth,
    diffusion,
):
    lat_count = lax.axis_size("lat")
    wave_count = lax.axis_size("wave")
    device_count = lat_count * wave_count
    local_rows = fourier.shape[0]
    local_pairs = legendre.shape[0]
    device_pos = lax.axis_index(("lat", "wave"))
    slot_wave = jnp.stack([pair_table, TRUNC - pair_table], axis=1).reshape(WAVES)
    picked = jnp.take(fourier, slot_wave, axis=1).reshape(
        local_rows, device_count, local_pairs, 2 * COLS
    )
    outgoing = jnp.transpose(picked, (1, 2, 0, 3))
    arrived = lax.all_to_all(
        outgoing.reshape(device_count, local_pairs, 1, local_rows, 2 * COLS),
        ("lat", "wave"),
        split_axis=0,
        concat_axis=2,
        tiled=True,
    )
    arrived = arrived.reshape(local_pairs, NLAT, 2, COLS)
    positions = jnp.arange(NLAT, dtype=jnp.int32)
    row_place = jnp.zeros((NLAT,), jnp.int32).at[row_lat].set(positions)
    northern = jnp.take(arrived, row_place[:NHALF], axis=1).astype(jnp.float32)
    southern = jnp.take(arrived, row_place[::-1][:NHALF], axis=1).astype(jnp.float32)
    folded = gauss_weight[None, :, None, None, None] * jnp.stack(
        [northern + southern, northern - southern], axis=3
    )
    folded = folded.astype(jnp.bfloat16).reshape(local_pairs, NHALF, 4 * COLS)
    own_orders = lax.dynamic_slice_in_dim(pair_table, device_pos * local_pairs, local_pairs)

    def run_pair(legendre_slab, folded_slab, order):
        return pair_step(
            legendre_slab, folded_slab, order, layer_pressure_matrix, modes, mode_depth, diffusion
        )

    placed, rebuilt = jax.vmap(run_pair, in_axes=(0, 0, 0))(legendre, folded, own_orders)
    spectrum = lax.psum_scatter(
        jnp.sum(placed, axis=0), ("lat", "wave"), scatter_dimension=0, tiled=True
    )
    stored = jnp.take(rebuilt, row_lat, axis=1)
    back = lax.all_to_all(
        stored.reshape(1, local_pairs, device_count, local_rows, 2 * COLS),
        ("lat", "wave"),
        split_axis=2,
        concat_axis=0,
        tiled=True,
    )
    back = back.reshape(device_count * local_pairs, local_rows, 2, COLS)
    back = jnp.transpose(back, (1, 0, 2, 3)).reshape(local_rows, WAVES, COLS)
    slot_of_wave = (
        jnp.zeros((WAVES,), jnp.int32).at[slot_wave].set(jnp.arange(WAVES, dtype=jnp.int32))
    )
    fourier_out = jnp.take(back, slot_of_wave, axis=1)
    return (fourier_out, spectrum)


def solution(mesh):
    placed = (
        P(("lat", "wave"), None, None),
        P(("lat", "wave"), None, None),
        P(),
        P(),
        P(),
        P(),
        P(),
        P(),
        P(),
    )
    return jax.shard_map(
        on_device,
        mesh=mesh,
        in_specs=placed,
        out_specs=(P(("lat", "wave"), None, None), P(("lat", "wave"), None)),
        check_vma=False,
    )
```

profile of v0, /device:TPU:0, one launch (start us, length us, event | category | flops | bytes accessed | tf_op | source)
XLA Modules:
  0.0 1673.7 jit_solution(12265951607006702049)
XLA Ops:
  9.0 37.6 %gather_fusion.1 = bf16[1280,40,128]{2,0,1:T(8,128)(2,1)} fusion(bf16[40,1280,128]{2,1,0:T(8,128)(2,1)} %param.13, s32[2048]{0:T(1024)S(1)} %pad_clamp_fusion.2), kind=kCustom, calls=%fused_computation.clone | custom fusion | bytes 26219520 | tf_op jit(solution)/shard_map/jit(_take)/gather | solution.py:112
  57.7 21.1 %reshape.523 = bf16[40,32,20,256]{3,2,1,0:T(8,128)(2,1)} reshape(bf16[40,1280,128]{2,1,0:T(8,128)(2,1)} %select_bitcast_fusion.1) | data formatting | bytes 26214400 | tf_op jit(solution)/shard_map/reshape | solution.py:112
  114.3 274.8 %all-to-all-done = bf16[32,20,1,40,256]{4,3,2,1,0:T(8,128)(2,1)} async-done(((bf16[32,20,1,40,256]{4,3,2,1,0:T(8,128)(2,1)}), bf16[32,20,1,40,256]{4,3,2,1,0:T(8,128)(2,1)}, u32[]{:S(2)}, u32[]{:S(2)}) %all-to-all-start) | async-done | bytes 13107232 | tf_op jit(solution)/shard_map/all_to_all | solution.py:116
  418.7 36.1 %gather_fusion.3 = bf16[640,20,2,128]{3,2,1,0:T(2,128)(2,1)} fusion(bf16[20,1280,2,128]{3,2,1,0:T(2,128)(2,1)} %reshape.525, s32[1024]{0:T(1024)S(1)} %pad_clamp_fusion.3), kind=kCustom, calls=%fused_computation.3.clone | custom fusion | bytes 13109760 | tf_op jit(solution)/shard_map/jit(_take)/gather | solution.py:127
  454.8 36.6 %gather_fusion.2 = bf16[640,20,2,128]{3,2,1,0:T(2,128)(2,1)} fusion(bf16[20,1280,2,128]{3,2,1,0:T(2,128)(2,1)} %reshape.525, s32[1024]{0:T(1024)S(1)} %pad_clamp_fusion.4), kind=kCustom, calls=%fused_computation.1.clone | custom fusion | bytes 13109760 | tf_op jit(solution)/shard_map/jit(_take)/gather | solution.py:126
  528.0 39.3 %copy.69 = f32[20,640,2,2,128]{1,4,3,2,0:T(8,128)} copy(f32[20,640,2,2,128]{4,2,0,1,3:T(2,128)} %pad_maximum_fusion.1) | data formatting | bytes 52428800 | tf_op jit(solution)/shard_map/stack | solution.py:128
  582.4 41.1 %convolution_bitcast_fusion = f32[20,1281,512]{2,1,0:T(8,128)} fusion(bf16[20,640,512]{1,2,0:T(8,128)(2,1)} %fusion, bf16[20,1281,640]{2,1,0:T(8,128)(2,1)} %param.14), kind=kOutput, calls=%fused_computation.9 | convolution fusion | flops 16790323200 | bytes 98370560 | tf_op jit(solution)/shard_map/vmap()/dot_general | solution.py:30
  623.5 45.4 %reshape.526 = f32[20,1281,4,128]{3,2,1,0:T(4,128)} reshape(f32[20,1281,512]{2,1,0:T(8,128)} %convolution_bitcast_fusion) | data formatting | bytes 104939520 | tf_op jit(solution)/shard_map/vmap()/reshape | solution.py:30
  668.8 82.0 %fusion.44 = (f32[20,1281,1,128]{3,2,1,0:T(1,128)}, f32[20,1281,1,128]{3,2,1,0:T(1,128)}, f32[20,1281,1,128]{3,2,1,0:T(1,128)}, f32[20,1281,1,128]{3,2,1,0:T(1,128)}) fusion(f32[20,1281,4,128]{3,2,1,0:T(4,128)} %reshape.526), kind=kLoop, calls=%fused_computation.116 | loop fusion | bytes 104939520 | tf_op jit(solution)/shard_map/vmap()/slice | solution.py:35
  750.8 29.5 %copy.105 = f32[20,1281,1,128]{1,3,0,2:T(8,128)} copy(f32[20,1281,1,128]{3,2,1,0:T(1,128)} %get-tuple-element.44) | data formatting | bytes 26234880
  780.3 29.7 %copy.106 = f32[20,1281,1,128]{1,3,0,2:T(8,128)} copy(f32[20,1281,1,128]{3,2,1,0:T(1,128)} %get-tuple-element.46) | data formatting | bytes 26234880
  810.0 29.5 %copy.107 = f32[20,1281,1,128]{1,3,0,2:T(8,128)} copy(f32[20,1281,1,128]{3,2,1,0:T(1,128)} %get-tuple-element.45) | data formatting | bytes 26234880
  839.5 29.5 %copy.108 = f32[20,1281,1,128]{1,3,0,2:T(8,128)} copy(f32[20,1281,1,128]{3,2,1,0:T(1,128)} %get-tuple-element.47) | data formatting | bytes 26234880
  928.7 20.0 %pad_maximum_fusion = bf16[20,1281,4,128]{1,3,0,2:T(8,128)(2,1)} fusion(bf16[20,1281,1,128]{1,3,0,2:T(8,128)(2,1)} %get-tuple-element.57, bf16[20,1281,1,128]{1,3,0,2:T(8,128)(2,1)} %get-tuple-element.58, bf16[20,1281,1,128]{1,3,0,2:T(8,128)(2,1)} %get-tuple-element.59, bf16[20,1281,1,128]{1,3,0,2:T(8,128)(2,1)} %get-tuple-element.56), kind=kLoop, calls=%fused_computation.10 | loop fusion | flops 39352320 | bytes 52469760 | tf_op jit(solution)/shard_map/vmap()/stack | solution.py:76
  948.7 44.5 %copy.82 = bf16[20,1281,4,128]{3,2,1,0:T(4,128)(2,1)} copy(bf16[20,1281,4,128]{1,3,0,2:T(8,128)(2,1)} %pad_maximum_fusion) | data formatting | bytes 52469760 | tf_op jit(solution)/shard_map/vmap()/stack | solution.py:76
  993.1 29.5 %reshape.527 = bf16[20,1281,512]{2,1,0:T(8,128)(2,1)} reshape(bf16[20,1281,4,128]{3,2,1,0:T(4,128)(2,1)} %copy.82) | data formatting | bytes 52469760 | tf_op jit(solution)/shard_map/vmap()/reshape | solution.py:84
  1022.6 35.9 %fusion.48 = f32[20,512,640]{2,1,0:T(8,128)} fusion(bf16[20,1281,512]{2,1,0:T(8,128)(2,1)} %reshape.527, bf16[20,1281,640]{2,1,0:T(8,128)(2,1)} %param.14), kind=kOutput, calls=%fused_computation.120 | convolution fusion | flops 16790323200 | bytes 85242880 | tf_op jit(solution)/shard_map/vmap()/dot_general | solution.py:85
  1075.3 19.9 %copy.109 = f32[20,640,2,1,128]{4,2,1,0,3:T(2,128)} copy(f32[20,640,2,1,128]{1,4,3,2,0:T(8,128)} %get-tuple-element.51) | data formatting | bytes 26214400
  1095.2 20.3 %copy.110 = f32[20,640,2,1,128]{4,2,1,0,3:T(2,128)} copy(f32[20,640,2,1,128]{1,4,3,2,0:T(8,128)} %get-tuple-element.50) | data formatting | bytes 26214400
  1141.0 57.6 %pad_maximum_fusion.2 = bf16[20,1280,2,128]{3,2,1,0:T(2,128)(2,1)} fusion(bf16[20,640,2,128]{3,2,1,0:T(2,128)(2,1)} %rev.4, bf16[20,640,2,128]{3,2,1,0:T(2,128)(2,1)} %get-tuple-element.48), kind=kLoop, calls=%fused_computation.22 | loop fusion | flops 6553600 | bytes 26214400 | tf_op jit(solution)/shard_map/vmap()/concatenate | solution.py:90
  1198.7 65.2 %gather_fusion = bf16[1280,20,2,128]{3,2,1,0:T(2,128)(2,1)} fusion(bf16[20,1280,2,128]{3,2,1,0:T(2,128)(2,1)} %pad_maximum_fusion.2, s32[2048]{0:T(1024)S(1)} %copy-done.15), kind=kCustom, calls=%fused_computation.4 | custom fusion | bytes 26219520 | tf_op jit(solution)/shard_map/jit(_take)/gather | solution.py:143
  1263.9 30.2 %reshape.629 = bf16[1,20,32,40,256]{4,1,3,2,0:T(8,128)(2,1)} reshape(bf16[20,1280,2,128]{3,2,0,1:T(2,128)(2,1)} %bitcast.104) | data formatting | bytes 26214400 | tf_op jit(solution)/shard_map/jit(_take)/gather | solution.py:143
  1338.0 73.2 %while.2 = (s32[]{:T(128)}, f32[20,2561,64]{1,2,0:T(8,128)}, s32[20,3]{0,1:T(4,128)S(1)}, f32[20,1280,64]{1,2,0:T(8,128)}) while((s32[]{:T(128)}, f32[20,2561,64]{1,2,0:T(8,128)}, s32[20,3]{0,1:T(4,128)S(1)}, f32[20,1280,64]{1,2,0:T(8,128)}) %tuple.57), condition=%wide.while_cond.clone, body=%wide.while_body.sunk.clone | while | flops 2 | bytes 656993 | solution.py:19
  1419.0 187.5 %all-to-all-done.1 = bf16[1,20,32,40,256]{4,3,1,0,2:T(8,128)(2,1)} async-done(((bf16[1,20,32,40,256]{4,3,1,0,2:T(8,128)(2,1)}), bf16[1,20,32,40,256]{4,3,1,0,2:T(8,128)(2,1)}, u32[]{:S(2)}, u32[]{:S(2)}) %all-to-all-start.1) | async-done | bytes 13107232 | tf_op jit(solution)/shard_map/all_to_all | solution.py:144
  (197 shorter events, 416.4 us)
Async XLA Ops:
  7.2 885.2 %copy-start = (f32[16,16]{1,0:T(8,128)S(1)}, f32[16,16]{1,0:T(8,128)}, u32[]{:S(2)}) copy-start(f32[16,16]{1,0:T(8,128)} %param.19) | copy-start | bytes 3076
  8.8 37.8 %copy-start.3 = (s32[640,2]{1,0:T(8,128)}, s32[640,2]{1,0:T(8,128)S(1)}, u32[]{:S(2)}) copy-start(s32[640,2]{1,0:T(8,128)S(1)} %copy.65) | copy-start | bytes 15364
  91.2 7.4 copy-start.16
  91.2 18.0 %copy-start.26 = (f32[16]{0:T(128)S(1)}, f32[16]{0:T(128)}, u32[]{:S(2)}) copy-start(f32[16]{0:T(128)} %param.20) | copy-start | bytes 196
  91.2 19.5 %copy-start.25 = (f32[4,16]{1,0:T(4,128)S(1)}, f32[4,16]{1,0:T(4,128)}, u32[]{:S(2)}) copy-start(f32[4,16]{1,0:T(4,128)} %param.21) | copy-start | bytes 772
  91.2 297.9 %all-to-all-start = ((bf16[32,20,1,40,256]{4,3,2,1,0:T(8,128)(2,1)}), bf16[32,20,1,40,256]{4,3,2,1,0:T(8,128)(2,1)}, u32[]{:S(2)}, u32[]{:S(2)}) async-start(bf16[32,20,1,40,256]{4,3,2,1,0:T(8,128)(2,1)} %copy.67), calls=%async_computation | async-start | bytes 26214400 | tf_op jit(solution)/shard_map/all_to_all | solution.py:116
  106.2 293.6 %copy-start.18 = (pred[1281]{0:T(1024)(128)(4,1)}, pred[1281]{0:T(1024)(128)(4,1)S(1)}, u32[]{:S(2)}) copy-start(pred[1281]{0:T(1024)(128)(4,1)S(1)} %get-tuple-element.73) | copy-start | bytes 3847
  106.9 293.0 %copy-start.21 = (s32[20]{0:T(128)}, s32[20]{0:T(128)S(1)}, u32[]{:S(2)}) copy-start(s32[20]{0:T(128)S(1)} %broadcast_subtract_fusion.1) | copy-start | bytes 244
  527.9 39.3 %copy-start.23 = (f32[640]{0:T(1024)S(1)}, f32[640]{0:T(1024)}, u32[]{:S(2)}) copy-start(f32[640]{0:T(1024)} %param.17) | copy-start | bytes 7684
  839.5 29.5 %copy-start.13 = (pred[20,1281]{1,0:T(8,128)(4,1)S(1)}, pred[20,1281]{1,0:T(8,128)(4,1)}, u32[]{:S(2)}) copy-start(pred[20,1281]{1,0:T(8,128)(4,1)} %get-tuple-element.68) | copy-start | bytes 76864
  839.5 29.5 %copy-start.14 = (pred[20,1281]{1,0:T(8,128)(4,1)S(1)}, pred[20,1281]{1,0:T(8,128)(4,1)}, u32[]{:S(2)}) copy-start(pred[20,1281]{1,0:T(8,128)(4,1)} %get-tuple-element.70) | copy-start | bytes 76864
  839.5 29.5 %copy-start.19 = (pred[1281]{0:T(1024)(128)(4,1)S(1)}, pred[1281]{0:T(1024)(128)(4,1)}, u32[]{:S(2)}) copy-start(pred[1281]{0:T(1024)(128)(4,1)} %copy-done.18) | copy-start | bytes 3847
  887.8 8.0 copy-start.5
  892.4 12.3 slice-start
  895.8 8.9 slice-start.1
  899.5 5.2 copy-start.2
  1141.0 57.6 %copy-start.15 = (s32[2048]{0:T(1024)S(1)}, s32[2048]{0:T(1024)}, u32[]{:S(2)}) copy-start(s32[2048]{0:T(1024)} %pad_clamp_fusion.1) | copy-start | bytes 24580
  1263.9 30.2 %copy-start.20 = (pred[32,40]{1,0:T(8,128)(4,1)S(1)}, pred[32,40]{1,0:T(8,128)(4,1)}, u32[]{:S(2)}) copy-start(pred[32,40]{1,0:T(8,128)(4,1)} %broadcast_in_dim.140) | copy-start | bytes 3844
  1307.9 9.7 copy-start.24
  1307.9 9.8 copy-start.22
  1307.9 298.6 %all-to-all-start.1 = ((bf16[1,20,32,40,256]{4,3,1,0,2:T(8,128)(2,1)}), bf16[1,20,32,40,256]{4,3,1,0,2:T(8,128)(2,1)}, u32[]{:S(2)}, u32[]{:S(2)}) async-start(bf16[1,20,32,40,256]{4,3,1,0,2:T(8,128)(2,1)} %copy.86), calls=%async_computation.1 | async-start | bytes 26214400 | tf_op jit(solution)/shard_map/all_to_all | solution.py:144
  1311.8 354.8 %reduce-scatter.5.cloned.1.call-start = ((), (), s32[]{:S(2)}) async-start(), calls=%async_computation.3 | async-start | bytes 675840
  1317.8 7.0 copy-start.8
  1649.6 17.1 %copy-start.1 = (f32[16,16]{1,0:T(8,128)S(1)}, f32[16,16]{1,0:T(8,128)}, u32[]{:S(2)}) copy-start(f32[16,16]{1,0:T(8,128)} %param.19) | copy-start | bytes 3076
  (8 other events, 23.2 us)
Sparse Core Ops, SparseCore 0:
  1419.2 171.7 reduce-scatter.4
where the time goes:
time: 1690 us; the launch traced here: 1670 us
  local copies, waits for them, and re-layouts  856 us (51%)
  waiting for transfers between devices  462 us (27%)
  other arithmetic  236 us (14%)
  matrix products  92.9 us (5%)
    all_to_all x1, waiting for transfers between devices, on_device(): lax.all_to_all(outgoing.reshape(device_count, local_pairs, 1, local_rows,...  275 us
    all_to_all x1, waiting for transfers between devices, on_device(): lax.all_to_all(stored.reshape(1, local_pairs, device_count, local_rows, 2...  187 us
    unnamed x66, local copies, waits for them, and re-layouts  168 us
    gather x2, local copies, waits for them, and re-layouts, on_device(): stored = jnp.take(rebuilt, row_lat, axis=1)  95.4 us
    slice x1, local copies, waits for them, and re-layouts, pair_step(): gathered[:, 1]  82 us
    gather x60, local copies, waits for them, and re-layouts  73.2 us
    concatenate x1, other arithmetic, pair_step(): rebuilt = jnp.concatenate([northern, southern[::-1]], axis=0)  57.6 us
    reshape x1, local copies, waits for them, and re-layouts, pair_step(): jnp.dot(legendre_slab, folded, preferred_element_type=jnp.float32)  45.4 us
  transfers between devices with their start and end apart: 3, of which 2 were waited for; matrix products, arithmetic and copies ran while one was open for 11% of the time, Pallas kernels for 0%

commit v1 on v0

v1 whole, which is shorter than its diff:
```python
import jax
import jax.numpy as jnp
from jax import lax
from jax.experimental import pallas as pl
from jax.experimental.pallas import tpu as pltpu
from jax.sharding import PartitionSpec as P

TRUNC = 1279
NLAT = 1280
FIELDS = 4
LEVELS = 16
WAVES = 1280
NPACK = 1281
NHALF = 640
COLS = 128
PITCH = 1288
KTILE = 256
NTAIL = 16
AXES = ("lat", "wave")
VMEM = 60 << 20
BF16 = jnp.bfloat16
F32 = jnp.float32


def divisor_up_to(number, most):
    return max(d for d in range(1, most + 1) if number % d == 0)


def gather_waves(pair_table, fourier, devices, local_pairs, first, count, padded):
    rows = fourier.shape[0]
    per_read = divisor_up_to(rows, 8)
    reads = rows // per_read
    per_write = divisor_up_to(devices, 4)

    def body(table, rows_ref, out_ref, held):
        step = pl.program_id(0)

        if padded > rows:

            @pl.when(step == 0)
            def _():
                held[rows * PITCH :, :] = jnp.zeros(((padded - rows) * PITCH, COLS), F32)

        @pl.when(step < reads)
        def _():
            for r in range(per_read):
                start = pl.multiple_of((step * per_read + r) * PITCH, 8)
                held[pl.ds(start, WAVES), :] = rows_ref[r].astype(F32)

        @pl.when(step >= reads)
        def _():
            def one_device(d, carry):
                for s in range(count):
                    wave = table[((step - reads) * per_write + d) * local_pairs + first + s]
                    both = jnp.concatenate(
                        [
                            held[pl.ds(wave, padded, stride=PITCH), :],
                            held[pl.ds(TRUNC - wave, padded, stride=PITCH), :],
                        ],
                        axis=0,
                    )
                    out_ref[d, pl.ds(s * 2 * padded, 2 * padded), :] = both.astype(BF16)
                return carry

            lax.fori_loop(0, per_write, one_device, 0)

    return pl.pallas_call(
        body,
        grid_spec=pltpu.PrefetchScalarGridSpec(
            num_scalar_prefetch=1,
            grid=(reads + devices // per_write,),
            in_specs=[
                pl.BlockSpec((per_read, WAVES, COLS), lambda i, t: (jnp.minimum(i, reads - 1), 0, 0))
            ],
            out_specs=pl.BlockSpec(
                (per_write, count * 2 * padded, COLS), lambda i, t: (jnp.maximum(i - reads, 0), 0, 0)
            ),
            scratch_shapes=[pltpu.VMEM((padded * PITCH, COLS), F32)],
        ),
        out_shape=jax.ShapeDtypeStruct((devices, count * 2 * padded, COLS), BF16),
        compiler_params=pltpu.CompilerParams(vmem_limit_bytes=VMEM),
        cost_estimate=pl.CostEstimate(flops=0, bytes_accessed=20_000_000, transcendentals=0),
        name="gather_waves",
    )(pair_table, fourier)


def scatter_waves(pair_table, chunks, spans, rows, devices, local_pairs, padded):
    per_read = divisor_up_to(devices, 4)
    reads = devices // per_read
    per_write = divisor_up_to(rows, 8)
    writes = rows // per_write

    def body(table, *refs):
        chunk_refs, out_ref, held = refs[: len(chunks)], refs[-2], refs[-1]
        step = pl.program_id(0)

        @pl.when(step < reads)
        def _():
            for (first, count), chunk_ref in zip(spans, chunk_refs):

                def one_device(d, carry, first=first, count=count, chunk_ref=chunk_ref):
                    for s in range(count):
                        wave = table[(step * per_read + d) * local_pairs + first + s]
                        both = chunk_ref[d, pl.ds(s * 2 * padded, 2 * padded), :].astype(F32)
                        held[pl.ds(wave, padded, stride=PITCH), :] = both[:padded]
                        held[pl.ds(TRUNC - wave, padded, stride=PITCH), :] = both[padded:]
                    return carry

                lax.fori_loop(0, per_read, one_device, 0)

        @pl.when(step >= reads)
        def _():
            for r in range(per_write):
                start = pl.multiple_of(((step - reads) * per_write + r) * PITCH, 8)
                out_ref[r] = held[pl.ds(start, WAVES), :].astype(BF16)

    return pl.pallas_call(
        body,
        grid_spec=pltpu.PrefetchScalarGridSpec(
            num_scalar_prefetch=1,
            grid=(reads + writes,),
            in_specs=[
                pl.BlockSpec(
                    (per_read, count * 2 * padded, COLS), lambda i, t: (jnp.minimum(i, reads - 1), 0, 0)
                )
                for _, count in spans
            ],
            out_specs=pl.BlockSpec(
                (per_write, WAVES, COLS), lambda i, t: (jnp.maximum(i - reads, 0), 0, 0)
            ),
            scratch_shapes=[pltpu.VMEM((padded * PITCH, COLS), F32)],
        ),
        out_shape=jax.ShapeDtypeStruct((rows, WAVES, COLS), BF16),
        compiler_params=pltpu.CompilerParams(vmem_limit_bytes=VMEM),
        cost_estimate=pl.CostEstimate(flops=0, bytes_accessed=26_000_000, transcendentals=0),
        name="scatter_waves",
    )(pair_table, *chunks)


def transform(orders, arrived, legendre, fold, unfold, weight, first_map, second_map, depth, damping, first, count, padded):
    devices = arrived.shape[0]
    all_rows = devices * padded

    def body(
        orders_ref, arrived_ref, legendre_ref, fold_ref, unfold_ref, weight_ref, map1_ref, map2_ref, depth_ref,
        damping_ref, out_ref, low_ref, high_ref, rows_in, folded, blocks, halves, tail,
    ):
        step = pl.program_id(0)
        order = orders_ref[first + step]

        @pl.when(step == 0)
        def _():
            low_ref[...] = jnp.zeros_like(low_ref)
            high_ref[...] = jnp.zeros_like(high_ref)
            tail[...] = jnp.zeros_like(tail)

        tail[0:1, :] = legendre_ref[0, NPACK - 1 : NPACK, :]

        arrived_rows = arrived_ref[...].astype(F32)
        rows_in[:, :COLS] = arrived_rows[:, :padded].reshape(all_rows, COLS).astype(BF16)
        rows_in[:, COLS:] = arrived_rows[:, padded:].reshape(all_rows, COLS).astype(BF16)

        def fold_tile(i, carry):
            at = pl.multiple_of(i * 128, 128)
            for part in range(2):
                sums = jnp.dot(
                    fold_ref[pl.ds(pl.multiple_of(part * NHALF + at, 128), 128), :],
                    rows_in[...],
                    preferred_element_type=F32,
                )
                folded[pl.ds(at, 128), part * 256 : part * 256 + 256] = (
                    weight_ref[pl.ds(at, 128), :] * sums
                ).astype(BF16)
            return carry

        lax.fori_loop(0, NHALF // 128, fold_tile, 0)

        def update(start, slab, size):
            gathered = jnp.dot(slab, folded[...], preferred_element_type=F32)
            packed = lax.broadcasted_iota(jnp.int32, (size, COLS), 0) + start
            in_first = packed <= TRUNC - order
            odd = jnp.where(in_first, packed, packed + order) % 2 == 1
            spectral = jnp.where(
                in_first,
                jnp.where(odd, gathered[:, 2 * COLS : 3 * COLS], gathered[:, :COLS]),
                jnp.where(odd, gathered[:, 3 * COLS :], gathered[:, COLS : 2 * COLS]),
            )
            degree = jnp.where(in_first, order + packed, packed - 1)
            scale = (degree * (degree + 1)).astype(F32) / F32(TRUNC * (TRUNC + 1))
            forced = jnp.dot(
                spectral, map1_ref[...], precision=lax.Precision.HIGHEST, preferred_element_type=F32
            )
            modal = (forced[:, :COLS] + scale * forced[:, COLS:]) / (1.0 + scale * depth_ref[...])
            evolved = jnp.dot(
                modal, map2_ref[...], precision=lax.Precision.HIGHEST, preferred_element_type=F32
            )
            field = (lax.broadcasted_iota(jnp.int32, (size, COLS), 1) // LEVELS) % FIELDS
            updated = (jnp.where(field == 1, 0.0, spectral) + evolved) / (
                1.0 + damping_ref[...] * (scale * scale)
            )
            energy = jnp.where(in_first & (order == 0), 1.0, 2.0) * (updated * updated)
            nothing = jnp.zeros_like(updated)
            for block, chosen in enumerate(
                (in_first & ~odd, ~in_first & ~odd, in_first & odd, ~in_first & odd)
            ):
                blocks[pl.ds(start, size), block * COLS : (block + 1) * COLS] = jnp.where(
                    chosen, updated, nothing
                ).astype(BF16)
            low = jnp.where(in_first, energy, nothing)
            high_ref[pl.ds(start, size), :] += energy - low
            return low

        def update_tile(i, carry):
            start = pl.multiple_of(i * KTILE, KTILE)
            low = update(start, legendre_ref[0, pl.ds(start, KTILE), :], KTILE)
            low_ref[pl.ds(start + order, KTILE), :] += low
            return carry

        lax.fori_loop(0, (NPACK - 1) // KTILE, update_tile, 0)
        update(NPACK - 1, tail[...], NTAIL)

        def synthesis_tile(i, carry):
            at = pl.multiple_of(i * 128, 128)
            both = lax.dot_general(
                legendre_ref[0, : NPACK - 1, pl.ds(at, 128)],
                blocks[: NPACK - 1, :],
                (((0,), (0,)), ((), ())),
                preferred_element_type=F32,
            ) + lax.dot_general(
                tail[:, pl.ds(at, 128)],
                blocks[NPACK - 1 :, :],
                (((0,), (0,)), ((), ())),
                preferred_element_type=F32,
            )
            halves[pl.ds(at, 128), :] = (both[:, :256] + both[:, 256:]).astype(BF16)
            halves[pl.ds(pl.multiple_of(NHALF + at, 128), 128), :] = (
                both[:, :256] - both[:, 256:]
            ).astype(BF16)
            return carry

        lax.fori_loop(0, NHALF // 128, synthesis_tile, 0)

        back = jnp.dot(unfold_ref[...], halves[...], preferred_element_type=F32)
        out_ref[...] = jnp.concatenate(
            [
                back[:, :COLS].reshape(devices, padded, COLS),
                back[:, COLS:].reshape(devices, padded, COLS),
            ],
            axis=1,
        ).astype(BF16)

    whole = lambda shape: pl.BlockSpec(shape, lambda i, t: (0,) * len(shape))
    return pl.pallas_call(
        body,
        grid_spec=pltpu.PrefetchScalarGridSpec(
            num_scalar_prefetch=1,
            grid=(count,),
            in_specs=[
                pl.BlockSpec((devices, 2 * padded, COLS), lambda i, t: (0, i, 0)),
                pl.BlockSpec((1, NPACK, NHALF), lambda i, t: (first + i, 0, 0)),
                whole(fold.shape),
                whole(unfold.shape),
                whole(weight.shape),
                whole(first_map.shape),
                whole(second_map.shape),
                whole(depth.shape),
                whole(damping.shape),
            ],
            out_specs=[
                pl.BlockSpec((devices, 2 * padded, COLS), lambda i, t: (0, i, 0)),
                whole((2 * WAVES, COLS)),
                whole((WAVES + NTAIL, COLS)),
            ],
            scratch_shapes=[
                pltpu.VMEM((all_rows, 2 * COLS), BF16),
                pltpu.VMEM((NHALF, 4 * COLS), BF16),
                pltpu.VMEM((WAVES + NTAIL, 4 * COLS), BF16),
                pltpu.VMEM((NLAT, 2 * COLS), BF16),
                pltpu.VMEM((NTAIL, NHALF), BF16),
            ],
        ),
        out_shape=[
            jax.ShapeDtypeStruct(arrived.shape, BF16),
            jax.ShapeDtypeStruct((2 * WAVES, COLS), F32),
            jax.ShapeDtypeStruct((WAVES + NTAIL, COLS), F32),
        ],
        compiler_params=pltpu.CompilerParams(vmem_limit_bytes=VMEM),
        cost_estimate=pl.CostEstimate(
            flops=count * 3_500_000_000, bytes_accessed=count * 3_000_000, transcendentals=0
        ),
        name="transform",
    )(orders, arrived, legendre, fold, unfold, weight, first_map, second_map, depth, damping)


def field_map(parts):
    one = jnp.zeros((FIELDS, LEVELS, FIELDS, LEVELS), F32)
    for source, target, matrix in parts:
        one = one.at[source, :, target, :].set(matrix)
    one = one.reshape(COLS // 2, COLS // 2)
    nothing = jnp.zeros_like(one)
    return jnp.concatenate(
        [jnp.concatenate([one, nothing], axis=1), jnp.concatenate([nothing, one], axis=1)], axis=0
    )


def on_device(
    fourier, legendre, pair_table, row_lat, gauss_weight, layer_pressure_matrix, modes, mode_depth, diffusion
):
    devices = lax.axis_size("lat") * lax.axis_size("wave")
    rows = fourier.shape[0]
    local_pairs = legendre.shape[0]
    padded = -(-rows // 8) * 8
    chunks = min(2, local_pairs)
    cuts = [local_pairs * c // chunks for c in range(chunks + 1)]
    spans = [(cuts[c], cuts[c + 1] - cuts[c]) for c in range(chunks)]
    own = lax.dynamic_slice_in_dim(
        pair_table, lax.axis_index(AXES) * local_pairs, local_pairs
    )

    lat = jnp.pad(
        row_lat.reshape(devices, rows), ((0, 0), (0, padded - rows)), constant_values=-1
    ).reshape(-1)
    half = jnp.arange(NHALF, dtype=jnp.int32)
    north_rows = (lat[None, :] == half[:, None]).astype(BF16)
    south_rows = (lat[None, :] == NLAT - 1 - half[:, None]).astype(BF16)
    fold = jnp.concatenate([north_rows + south_rows, north_rows - south_rows], axis=0)
    unfold = jnp.concatenate(
        [lat[:, None] == half[None, :], lat[:, None] == NLAT - 1 - half[None, :]], axis=1
    ).astype(BF16)
    high = lax.Precision.HIGHEST
    first_map = jnp.concatenate(
        [
            field_map([(1, 1, modes)]),
            field_map([(2, 1, jnp.dot(layer_pressure_matrix, modes, precision=high))]),
        ],
        axis=1,
    )
    second_map = field_map(
        [
            (1, 1, modes.T),
            (1, 2, -jnp.dot(modes.T, layer_pressure_matrix.T, precision=high)),
        ]
    )
    depth = jnp.tile(
        jnp.zeros((FIELDS, LEVELS), F32).at[1].set(mode_depth).reshape(1, -1), (1, 2)
    )
    damping = jnp.tile(diffusion.reshape(1, -1), (1, 2))

    outgoing = [
        gather_waves(pair_table, fourier, devices, local_pairs, first, count, padded)
        for first, count in spans
    ]
    arrived = [lax.all_to_all(block, AXES, 0, 0, tiled=True) for block in outgoing]
    done = [
        transform(
            own, block, legendre, fold, unfold, gauss_weight.reshape(NHALF, 1), first_map, second_map,
            depth, damping, first, count, padded,
        )
        for block, (first, count) in zip(arrived, spans)
    ]
    energy = sum(low[:WAVES] + high[1 : WAVES + 1] for _, low, high in done)
    spectrum = lax.psum_scatter(
        energy[:, : COLS // 2] + energy[:, COLS // 2 :], AXES, scatter_dimension=0, tiled=True
    )
    back = [lax.all_to_all(block, AXES, 0, 0, tiled=True) for block, _, _ in done]
    fourier_out = scatter_waves(pair_table, back, spans, rows, devices, local_pairs, padded)
    return (fourier_out, spectrum)


def solution(mesh):
    split = P(AXES, None, None)
    placed = (split, split, P(), P(), P(), P(), P(), P(), P())
    return jax.shard_map(
        on_device,
        mesh=mesh,
        in_specs=placed,
        out_specs=(split, P(AXES, None)),
        check_vma=False,
    )
```

time: 1690 us -> 651 us (0.39)
  local copies, waits for them, and re-layouts: 856 us -> 4.25 us
  Pallas kernels: 0 us -> 296 us
  other arithmetic: 236 us -> 9.99 us
  waiting for transfers between devices: 462 us -> 304 us
  matrix products: 92.9 us -> 0.33 us
    pallas_call x0 -> x5, Pallas kernels: none -> 296 us  [the longest x2 254 us: transform(): pl.pallas_call(body, grid_spec=pltpu.PrefetchScalarGridSpec(num_scalar_pr...]
    gather x66 -> x0, local copies, waits for them, and re-layouts: 291 us -> none  [the longest x2 95.4 us: on_device(): stored = jnp.take(rebuilt, row_lat, axis=1)]
    unnamed x66 -> x20, local copies, waits for them, and re-layouts: 168 us -> 0.05 us
    all_to_all x2 -> x4, waiting for transfers between devices: 462 us -> 304 us  [on_device(): lax.all_to_all(block, AXES, 0, 0, tiled=True)]
    reshape x8 -> x4, local copies, waits for them, and re-layouts: 146 us -> 1.21 us  [the longest x1 0.86 us: on_device(): gauss_weight.reshape(NHALF, 1)]
    slice x4 -> x0, local copies, waits for them, and re-layouts: 99.3 us -> none  [the longest x1 82 us: pair_step(): gathered[:, 1]]
    dot_general x6 -> x2, matrix products: 92.9 us -> 0.33 us  [the longest x1 0.19 us: on_device(): jnp.dot(modes.T, layer_pressure_matrix.T, precision=high)]
    another operation x5 -> x7, local copies, waits for them, and re-layouts: 84.6 us -> 1.54 us  [the longest x3 0.76 us: on_device(): damping = jnp.tile(diffusion.reshape(1, -1), (1, 2))]
  transfers between devices with their start and end apart: 3 -> 5, of which waited for: 2 -> 4; matrix products, arithmetic and copies ran while one was open for 11% -> 2% of each run, Pallas kernels for 0% -> 44%
where the time goes in v1:
time: 651 us; the launch traced here: 647 us
  waiting for transfers between devices  304 us (47%)
  Pallas kernels  296 us (45%)
  starting transfers between devices  18.5 us (3%)
  between operations  14.2 us (2%)
  other arithmetic  9.99 us (2%)
    all_to_all x4, waiting for transfers between devices, on_device(): lax.all_to_all(block, AXES, 0, 0, tiled=True)  304 us
    pallas_call x2, Pallas kernels, transform(): pl.pallas_call(body, grid_spec=pltpu.PrefetchScalarGridSpec(num_scalar_pr...  254 us
    pallas_call x2, Pallas kernels, gather_waves(): pl.pallas_call(body, grid_spec=pltpu.PrefetchScalarGridSpec(num_scalar_pr...  26.6 us
    all_to_all x4, starting transfers between devices, on_device(): lax.all_to_all(block, AXES, 0, 0, tiled=True)  18.4 us
    pallas_call x1, Pallas kernels, scatter_waves(): pl.pallas_call(body, grid_spec=pltpu.PrefetchScalarGridSpec(num_scalar_pr...  15.2 us
  transfers between devices with their start and end apart: 5, of which 4 were waited for; matrix products, arithmetic and copies ran while one was open for 2% of the time, Pallas kernels for 44%

profile of v1, /device:TPU:0, one launch (start us, length us, event | category | flops | bytes accessed | tf_op | source)
XLA Modules:
  0.0 647.1 jit_solution(18143040682369512371)
XLA Ops:
  7.2 13.4 %gather_waves.3 = bf16[32,800,128]{2,1,0:T(8,128)(2,1)} custom-call(s32[640]{0:T(1024)} %table.5, bf16[40,1280,128]{2,1,0:T(8,128)(2,1)} %rows_ref.3), custom_call_target="tpu_custom_call" | custom-call | bytes 20000000 | tf_op jit(solution)/shard_map/gather_waves/pallas_call | solution.py:67
  20.6 7.4 %all-to-all-start.2 = ((bf16[32,800,128]{2,1,0:T(8,128)(2,1)}), bf16[32,800,128]{2,1,0:T(8,128)(2,1)}, u32[]{:S(2)}, u32[]{:S(2)}) async-start(bf16[32,800,128]{2,1,0:T(8,128)(2,1)} %gather_waves.3), calls=%async_computation.2 | async-start | bytes 13107200 | tf_op jit(solution)/shard_map/all_to_all | solution.py:353
  28.0 13.1 %gather_waves.2 = bf16[32,800,128]{2,1,0:T(8,128)(2,1)} custom-call(s32[640]{0:T(1024)} %table.5, bf16[40,1280,128]{2,1,0:T(8,128)(2,1)} %rows_ref.3), custom_call_target="tpu_custom_call" | custom-call | bytes 20000000 | tf_op jit(solution)/shard_map/gather_waves/pallas_call | solution.py:67
  41.2 132.7 %all-to-all-done.2.arrived_ref = bf16[32,800,128]{2,1,0:T(8,128)(2,1)} async-done(((bf16[32,800,128]{2,1,0:T(8,128)(2,1)}), bf16[32,800,128]{2,1,0:T(8,128)(2,1)}, u32[]{:S(2)}, u32[]{:S(2)}) %all-to-all-start.2) | async-done | bytes 6553632 | tf_op jit(solution)/shard_map/all_to_all | solution.py:353
  173.9 3.6 all-to-all-start
  177.5 1.3 dynamic_slice.3.orders_ref
  178.9 0.7 tile.25.damping_ref
  181.2 0.9 reshape.234.weight_ref
  182.1 0.7 select_maximum_fusion.2.map2_ref
  182.8 0.7 fusion.4.map1_ref
  183.6 0.8 fusion.2
  184.4 1.0 iota_compare_fusion
  185.3 2.5 add_convert_fusion.unfold_ref
  187.8 1.9 pad_maximum_fusion.fold_ref
  189.8 127.0 %transform.3 = (bf16[32,800,128]{2,1,0:T(8,128)(2,1)}, f32[2560,128]{1,0:T(8,128)}, f32[1296,128]{1,0:T(8,128)}) custom-call(s32[20]{0:T(128)} %dynamic_slice.3.orders_ref, bf16[32,800,128]{2,1,0:T(8,128)(2,1)} %all-to-all-done.2.arrived_ref, bf16[20,1281,640]{2,1,0:T(8,128)(2,1)} %legendre_ref.3, bf16[1280,1280]{1,0:T(8,128)(2,1)} %pad_maximum_fusion.fold_ref, ...), custom_call_target="tpu_custom_call" | custom-call | flops 35000000512 | bytes 30000000 | tf_op jit(solution)/shard_map/transform/pallas_call | solution.py:253
  316.8 6.5 all-to-all-done.arrived_ref
  323.2 3.6 all-to-all-start.3
  326.9 126.9 %transform.2 = (bf16[32,800,128]{2,1,0:T(8,128)(2,1)}, f32[2560,128]{1,0:T(8,128)}, f32[1296,128]{1,0:T(8,128)}) custom-call(s32[20]{0:T(128)} %dynamic_slice.3.orders_ref, bf16[32,800,128]{2,1,0:T(8,128)(2,1)} %all-to-all-done.arrived_ref, bf16[20,1281,640]{2,1,0:T(8,128)(2,1)} %legendre_ref.3, bf16[1280,1280]{1,0:T(8,128)(2,1)} %pad_maximum_fusion.fold_ref, ...), custom_call_target="tpu_custom_call" | custom-call | flops 35000000512 | bytes 30000000 | tf_op jit(solution)/shard_map/transform/pallas_call | solution.py:253
  453.8 18.8 %all-to-all-done.3.refs_1_ = bf16[32,800,128]{2,1,0:T(8,128)(2,1)} async-done(((bf16[32,800,128]{2,1,0:T(8,128)(2,1)}), bf16[32,800,128]{2,1,0:T(8,128)(2,1)}, u32[]{:S(2)}, u32[]{:S(2)}) %all-to-all-start.3) | async-done | bytes 6553632 | tf_op jit(solution)/shard_map/all_to_all | solution.py:365
  472.6 3.8 all-to-all-start.1
  476.5 1.3 add_add_fusion
  477.8 1.1 slice_add_fusion
  478.9 146.2 %all-to-all-done.1.refs_0_ = bf16[32,800,128]{2,1,0:T(8,128)(2,1)} async-done(((bf16[32,800,128]{2,1,0:T(8,128)(2,1)}), bf16[32,800,128]{2,1,0:T(8,128)(2,1)}, u32[]{:S(2)}, u32[]{:S(2)}) %all-to-all-start.1) | async-done | bytes 6553632 | tf_op jit(solution)/shard_map/all_to_all | solution.py:365
  625.1 15.2 %scatter_waves.1 = bf16[40,1280,128]{2,1,0:T(8,128)(2,1)} custom-call(s32[640]{0:T(1024)} %table.5, bf16[32,800,128]{2,1,0:T(8,128)(2,1)} %all-to-all-done.1.refs_0_, bf16[32,800,128]{2,1,0:T(8,128)(2,1)} %all-to-all-done.3.refs_1_), custom_call_target="tpu_custom_call" | custom-call | bytes 26000000 | tf_op jit(solution)/shard_map/scatter_waves/pallas_call | solution.py:117
  (41 shorter events, 1.8 us)
Async XLA Ops:
  7.2 173.1 %copy-start = (f32[16,16]{1,0:T(8,128)S(1)}, f32[16,16]{1,0:T(8,128)}, u32[]{:S(2)}) copy-start(f32[16,16]{1,0:T(8,128)} %param.24) | copy-start | bytes 3076
  20.6 153.2 %all-to-all-start.2 = ((bf16[32,800,128]{2,1,0:T(8,128)(2,1)}), bf16[32,800,128]{2,1,0:T(8,128)(2,1)}, u32[]{:S(2)}, u32[]{:S(2)}) async-start(bf16[32,800,128]{2,1,0:T(8,128)(2,1)} %gather_waves.3), calls=%async_computation.2 | async-start | bytes 13107200 | tf_op jit(solution)/shard_map/all_to_all | solution.py:353
  41.2 137.6 %copy-start.8 = (f32[4,16]{1,0:T(4,128)S(1)}, f32[4,16]{1,0:T(4,128)}, u32[]{:S(2)}) copy-start(f32[4,16]{1,0:T(4,128)} %param.27) | copy-start | bytes 772
  41.2 138.4 %copy-start.9 = (f32[16]{0:T(128)S(1)}, f32[16]{0:T(128)}, u32[]{:S(2)}) copy-start(f32[16]{0:T(128)} %param.26) | copy-start | bytes 196
  41.2 139.1 %copy-start.5 = (f32[16,16]{1,0:T(8,128)S(1)}, f32[16,16]{1,0:T(8,128)}, u32[]{:S(2)}) copy-start(f32[16,16]{1,0:T(8,128)} %param.25) | copy-start | bytes 3076
  41.2 140.1 %copy-start.7 = (f32[640]{0:T(1024)S(1)}, f32[640]{0:T(1024)}, u32[]{:S(2)}) copy-start(f32[640]{0:T(1024)} %param.23) | copy-start | bytes 7684
  41.2 142.4 %copy-start.6 = (s32[1280]{0:T(1024)S(1)}, s32[1280]{0:T(1024)}, u32[]{:S(2)}) copy-start(s32[1280]{0:T(1024)} %param.22) | copy-start | bytes 15364
  173.9 149.4 %all-to-all-start = ((bf16[32,800,128]{2,1,0:T(8,128)(2,1)}), bf16[32,800,128]{2,1,0:T(8,128)(2,1)}, u32[]{:S(2)}, u32[]{:S(2)}) async-start(bf16[32,800,128]{2,1,0:T(8,128)(2,1)} %gather_waves.2), calls=%async_computation | async-start | bytes 13107200 | tf_op jit(solution)/shard_map/all_to_all | solution.py:353
  323.2 149.4 %all-to-all-start.3 = ((bf16[32,800,128]{2,1,0:T(8,128)(2,1)}), bf16[32,800,128]{2,1,0:T(8,128)(2,1)}, u32[]{:S(2)}, u32[]{:S(2)}) async-start(bf16[32,800,128]{2,1,0:T(8,128)(2,1)} %get-tuple-element.69), calls=%async_computation.3 | async-start | bytes 13107200 | tf_op jit(solution)/shard_map/all_to_all | solution.py:365
  472.6 3.8 copy-start.2
  472.6 3.9 copy-start.3
  472.6 3.9 copy-start.4
  472.6 152.4 %all-to-all-start.1 = ((bf16[32,800,128]{2,1,0:T(8,128)(2,1)}), bf16[32,800,128]{2,1,0:T(8,128)(2,1)}, u32[]{:S(2)}, u32[]{:S(2)}) async-start(bf16[32,800,128]{2,1,0:T(8,128)(2,1)} %get-tuple-element.68), calls=%async_computation.1 | async-start | bytes 13107200 | tf_op jit(solution)/shard_map/all_to_all | solution.py:365
  476.4 163.9 %reduce-scatter.5.cloned.1.call-start = ((), (), s32[]{:S(2)}) async-start(), calls=%async_computation.5 | async-start | bytes 675840
  625.1 15.2 %copy-start.1 = (f32[16,16]{1,0:T(8,128)S(1)}, f32[16,16]{1,0:T(8,128)}, u32[]{:S(2)}) copy-start(f32[16,16]{1,0:T(8,128)} %param.24) | copy-start | bytes 3076
Sparse Core Ops, SparseCore 0:
  480.1 145.1 reduce-scatter.4

commit v2 on v1

--- a/solution.py
+++ b/solution.py
@@ -301,6 +301,21 @@
     return jnp.concatenate(
         [jnp.concatenate([one, nothing], axis=1), jnp.concatenate([nothing, one], axis=1)], axis=0
     )
+
+
+def scatter_sum(parts, devices):
+    device = lax.axis_index(AXES)
+    rows, columns = parts.shape[0] // devices, parts.shape[1]
+    sums = parts.reshape(devices, rows * columns // COLS, COLS)
+    bit = 1
+    while bit < devices:
+        sums = sums.reshape((sums.shape[0] // 2, 2) + sums.shape[1:])
+        own = (device // bit) % 2
+        kept = lax.dynamic_index_in_dim(sums, own, 1, keepdims=False)
+        sent = lax.dynamic_index_in_dim(sums, 1 - own, 1, keepdims=False)
+        sums = kept + lax.ppermute(sent, AXES, [(d, d ^ bit) for d in range(devices)])
+        bit *= 2
+    return sums.reshape(rows, columns)
 
 
 def on_device(
@@ -359,9 +374,7 @@
         for block, (first, count) in zip(arrived, spans)
     ]
     energy = sum(low[:WAVES] + high[1 : WAVES + 1] for _, low, high in done)
-    spectrum = lax.psum_scatter(
-        energy[:, : COLS // 2] + energy[:, COLS // 2 :], AXES, scatter_dimension=0, tiled=True
-    )
+    spectrum = scatter_sum(energy[:, : COLS // 2] + energy[:, COLS // 2 :], devices)
     back = [lax.all_to_all(block, AXES, 0, 0, tiled=True) for block, _, _ in done]
     fourier_out = scatter_waves(pair_table, back, spans, rows, devices, local_pairs, padded)
     return (fourier_out, spectrum)

time: 651 us -> 632 us (0.971)
  between operations: 14.2 us -> 0.95 us
  waiting for transfers between devices: 304 us -> 294 us
  starting transfers between devices: 18.5 us -> 25.8 us
    all_to_all x4, waiting for transfers between devices: 304 us -> 158 us  [on_device(): lax.all_to_all(block, AXES, 0, 0, tiled=True)]
    ppermute x0 -> x5, waiting for transfers between devices: none -> 136 us  [scatter_sum(): lax.ppermute(sent, AXES, [(d, d ^ bit) for d in range(devices)])]
    ppermute x0 -> x5, starting transfers between devices: none -> 7.36 us  [scatter_sum(): lax.ppermute(sent, AXES, [(d, d ^ bit) for d in range(devices)])]
  transfers between devices with their start and end apart: 5 -> 9, of which waited for: 4 -> 8; matrix products, arithmetic and copies ran while one was open for 2% -> 2% of each run, Pallas kernels for 44% -> 42%
where the time goes in v2:
time: 632 us
  Pallas kernels  296 us (47%)
  waiting for transfers between devices  294 us (47%)
  starting transfers between devices  25.8 us (4%)
  other arithmetic  9.23 us (1%)
    pallas_call x2, Pallas kernels, transform(): pl.pallas_call(body, grid_spec=pltpu.PrefetchScalarGridSpec(num_scalar_pr...  254 us
    all_to_all x4, waiting for transfers between devices, on_device(): lax.all_to_all(block, AXES, 0, 0, tiled=True)  158 us
    ppermute x5, waiting for transfers between devices, scatter_sum(): lax.ppermute(sent, AXES, [(d, d ^ bit) for d in range(devices)])  136 us
    pallas_call x2, Pallas kernels, gather_waves(): pl.pallas_call(body, grid_spec=pltpu.PrefetchScalarGridSpec(num_scalar_pr...  26.5 us
    all_to_all x4, starting transfers between devices, on_device(): lax.all_to_all(block, AXES, 0, 0, tiled=True)  18.5 us
    pallas_call x1, Pallas kernels, scatter_waves(): pl.pallas_call(body, grid_spec=pltpu.PrefetchScalarGridSpec(num_scalar_pr...  15.2 us
  transfers between devices with their start and end apart: 9, of which 8 were waited for; matrix products, arithmetic and copies ran while one was open for 2% of the time, Pallas kernels for 42%

profile of v2, /device:TPU:0, one launch (start us, length us, event | category | flops | bytes accessed | tf_op | source)
XLA Modules:
  0.0 631.8 jit_solution(4186205766293459102)
XLA Ops:
  0.6 13.3 %gather_waves.2 = bf16[32,800,128]{2,1,0:T(8,128)(2,1)} custom-call(s32[640]{0:T(1024)} %table.5, bf16[40,1280,128]{2,1,0:T(8,128)(2,1)} %rows_ref.3), custom_call_target="tpu_custom_call" | custom-call | bytes 20000000 | tf_op jit(solution)/shard_map/gather_waves/pallas_call | solution.py:67
  13.9 7.4 %all-to-all-start = ((bf16[32,800,128]{2,1,0:T(8,128)(2,1)}), bf16[32,800,128]{2,1,0:T(8,128)(2,1)}, u32[]{:S(2)}, u32[]{:S(2)}) async-start(bf16[32,800,128]{2,1,0:T(8,128)(2,1)} %gather_waves.2), calls=%async_computation | async-start | bytes 13107200 | tf_op jit(solution)/shard_map/all_to_all | solution.py:368
  21.3 13.2 %gather_waves.3 = bf16[32,800,128]{2,1,0:T(8,128)(2,1)} custom-call(s32[640]{0:T(1024)} %table.5, bf16[40,1280,128]{2,1,0:T(8,128)(2,1)} %rows_ref.3), custom_call_target="tpu_custom_call" | custom-call | bytes 20000000 | tf_op jit(solution)/shard_map/gather_waves/pallas_call | solution.py:67
  34.6 132.6 %all-to-all-done.arrived_ref = bf16[32,800,128]{2,1,0:T(8,128)(2,1)} async-done(((bf16[32,800,128]{2,1,0:T(8,128)(2,1)}), bf16[32,800,128]{2,1,0:T(8,128)(2,1)}, u32[]{:S(2)}, u32[]{:S(2)}) %all-to-all-start) | async-done | bytes 6553632 | tf_op jit(solution)/shard_map/all_to_all | solution.py:368
  167.2 3.6 all-to-all-start.2
  170.8 1.3 dynamic_slice.34.orders_ref
  178.6 1.9 pad_maximum_fusion.fold_ref
  180.5 2.4 add_convert_fusion.unfold_ref
  183.0 126.9 %transform.2 = (bf16[32,800,128]{2,1,0:T(8,128)(2,1)}, f32[2560,128]{1,0:T(8,128)}, f32[1296,128]{1,0:T(8,128)}) custom-call(s32[20]{0:T(128)} %dynamic_slice.34.orders_ref, bf16[32,800,128]{2,1,0:T(8,128)(2,1)} %all-to-all-done.arrived_ref, bf16[20,1281,640]{2,1,0:T(8,128)(2,1)} %legendre_ref.3, bf16[1280,1280]{1,0:T(8,128)(2,1)} %pad_maximum_fusion.fold_ref, ...), custom_call_target="tpu_custom_call" | custom-call | flops 35000000512 | bytes 30000000 | tf_op jit(solution)/shard_map/transform/pallas_call | solution.py:253
  309.9 6.7 %all-to-all-done.2.arrived_ref = bf16[32,800,128]{2,1,0:T(8,128)(2,1)} async-done(((bf16[32,800,128]{2,1,0:T(8,128)(2,1)}), bf16[32,800,128]{2,1,0:T(8,128)(2,1)}, u32[]{:S(2)}, u32[]{:S(2)}) %all-to-all-start.2) | async-done | bytes 6553632 | tf_op jit(solution)/shard_map/all_to_all | solution.py:368
  316.5 3.6 all-to-all-start.1
  320.2 127.0 %transform.3 = (bf16[32,800,128]{2,1,0:T(8,128)(2,1)}, f32[2560,128]{1,0:T(8,128)}, f32[1296,128]{1,0:T(8,128)}) custom-call(s32[20]{0:T(128)} %dynamic_slice.34.orders_ref, bf16[32,800,128]{2,1,0:T(8,128)(2,1)} %all-to-all-done.2.arrived_ref, bf16[20,1281,640]{2,1,0:T(8,128)(2,1)} %legendre_ref.3, bf16[1280,1280]{1,0:T(8,128)(2,1)} %pad_maximum_fusion.fold_ref, ...), custom_call_target="tpu_custom_call" | custom-call | flops 35000000512 | bytes 30000000 | tf_op jit(solution)/shard_map/transform/pallas_call | solution.py:253
  447.2 18.7 %all-to-all-done.1.refs_0_ = bf16[32,800,128]{2,1,0:T(8,128)(2,1)} async-done(((bf16[32,800,128]{2,1,0:T(8,128)(2,1)}), bf16[32,800,128]{2,1,0:T(8,128)(2,1)}, u32[]{:S(2)}, u32[]{:S(2)}) %all-to-all-start.1) | async-done | bytes 6553632 | tf_op jit(solution)/shard_map/all_to_all | solution.py:378
  465.9 3.8 all-to-all-start.3
  469.8 1.3 add_add_fusion
  471.7 1.3 collective-permute-done
  473.2 1.6 collective-permute-start.1
  474.9 42.3 %collective-permute-done.1 = f32[8,20,128]{2,0,1:T(8,128)S(1)} collective-permute-done((f32[8,20,128]{2,0,1:T(8,128)S(1)}, f32[8,20,128]{2,0,1:T(8,128)S(1)}, u32[]{:S(2)}, u32[]{:S(2)}) %collective-permute-start.1) | collective-permute-done | bytes 81952 | tf_op jit(solution)/shard_map/ppermute | solution.py:316
  517.4 4.0 collective-permute-done.2
  521.4 1.4 collective-permute-start.3
  522.9 54.9 %collective-permute-done.3 = f32[2,20,128]{2,0,1:T(2,128)S(1)} collective-permute-done((f32[2,20,128]{2,0,1:T(2,128)S(1)}, f32[2,20,128]{2,0,1:T(2,128)S(1)}, u32[]{:S(2)}, u32[]{:S(2)}) %collective-permute-start.3) | collective-permute-done | bytes 20512 | tf_op jit(solution)/shard_map/ppermute | solution.py:316
  577.8 4.1 collective-permute-start.4
  581.9 34.0 %collective-permute-done.4 = f32[1,20,128]{2,0,1:T(1,128)S(1)} collective-permute-done((f32[1,20,128]{2,0,1:T(1,128)S(1)}, f32[1,20,128]{2,0,1:T(1,128)S(1)}, u32[]{:S(2)}, u32[]{:S(2)}) %collective-permute-start.4) | collective-permute-done | bytes 10272 | tf_op jit(solution)/shard_map/ppermute | solution.py:316
  616.6 15.2 %scatter_waves.1 = bf16[40,1280,128]{2,1,0:T(8,128)(2,1)} custom-call(s32[640]{0:T(1024)} %table.5, bf16[32,800,128]{2,1,0:T(8,128)(2,1)} %all-to-all-done.1.refs_0_, bf16[32,800,128]{2,1,0:T(8,128)(2,1)} %all-to-all-done.3.refs_1_), custom_call_target="tpu_custom_call" | custom-call | bytes 26000000 | tf_op jit(solution)/shard_map/scatter_waves/pallas_call | solution.py:117
  (61 shorter events, 8.2 us)
Async XLA Ops:
  0.6 172.3 %copy-start = (f32[16,16]{1,0:T(8,128)S(1)}, f32[16,16]{1,0:T(8,128)}, u32[]{:S(2)}) copy-start(f32[16,16]{1,0:T(8,128)} %param.24) | copy-start | bytes 3076
  13.9 153.2 %all-to-all-start = ((bf16[32,800,128]{2,1,0:T(8,128)(2,1)}), bf16[32,800,128]{2,1,0:T(8,128)(2,1)}, u32[]{:S(2)}, u32[]{:S(2)}) async-start(bf16[32,800,128]{2,1,0:T(8,128)(2,1)} %gather_waves.2), calls=%async_computation | async-start | bytes 13107200 | tf_op jit(solution)/shard_map/all_to_all | solution.py:368
  34.5 137.5 %copy-start.7 = (f32[640]{0:T(1024)S(1)}, f32[640]{0:T(1024)}, u32[]{:S(2)}) copy-start(f32[640]{0:T(1024)} %param.23) | copy-start | bytes 7684
  34.5 138.4 %copy-start.5 = (f32[16,16]{1,0:T(8,128)S(1)}, f32[16,16]{1,0:T(8,128)}, u32[]{:S(2)}) copy-start(f32[16,16]{1,0:T(8,128)} %param.25) | copy-start | bytes 3076
  34.6 139.4 %copy-start.9 = (f32[16]{0:T(128)S(1)}, f32[16]{0:T(128)}, u32[]{:S(2)}) copy-start(f32[16]{0:T(128)} %param.26) | copy-start | bytes 196
  34.6 140.0 %copy-start.8 = (f32[4,16]{1,0:T(4,128)S(1)}, f32[4,16]{1,0:T(4,128)}, u32[]{:S(2)}) copy-start(f32[4,16]{1,0:T(4,128)} %param.27) | copy-start | bytes 772
  34.6 142.2 %copy-start.6 = (s32[1280]{0:T(1024)S(1)}, s32[1280]{0:T(1024)}, u32[]{:S(2)}) copy-start(s32[1280]{0:T(1024)} %param.22) | copy-start | bytes 15364
  167.2 149.4 %all-to-all-start.2 = ((bf16[32,800,128]{2,1,0:T(8,128)(2,1)}), bf16[32,800,128]{2,1,0:T(8,128)(2,1)}, u32[]{:S(2)}, u32[]{:S(2)}) async-start(bf16[32,800,128]{2,1,0:T(8,128)(2,1)} %gather_waves.3), calls=%async_computation.2 | async-start | bytes 13107200 | tf_op jit(solution)/shard_map/all_to_all | solution.py:368
  316.5 149.4 %all-to-all-start.1 = ((bf16[32,800,128]{2,1,0:T(8,128)(2,1)}), bf16[32,800,128]{2,1,0:T(8,128)(2,1)}, u32[]{:S(2)}, u32[]{:S(2)}) async-start(bf16[32,800,128]{2,1,0:T(8,128)(2,1)} %get-tuple-element.68), calls=%async_computation.1 | async-start | bytes 13107200 | tf_op jit(solution)/shard_map/all_to_all | solution.py:378
  465.9 3.8 copy-start.2
  465.9 3.8 copy-start.3
  465.9 3.8 copy-start.4
  465.9 150.6 %all-to-all-start.3 = ((bf16[32,800,128]{2,1,0:T(8,128)(2,1)}), bf16[32,800,128]{2,1,0:T(8,128)(2,1)}, u32[]{:S(2)}, u32[]{:S(2)}) async-start(bf16[32,800,128]{2,1,0:T(8,128)(2,1)} %get-tuple-element.69), calls=%async_computation.3 | async-start | bytes 13107200 | tf_op jit(solution)/shard_map/all_to_all | solution.py:378
  471.6 1.5 collective-permute-start
  473.2 44.0 %collective-permute-start.1 = (f32[8,20,128]{2,0,1:T(8,128)S(1)}, f32[8,20,128]{2,0,1:T(8,128)S(1)}, u32[]{:S(2)}, u32[]{:S(2)}) collective-permute-start(f32[8,20,128]{2,0,1:T(8,128)S(1)} %bitcast.38), channel_id=1, source_target_pairs={{0,2},{1,3},{2,0},{3,1},{4,6},{5,7},{6,4},{7,5},{8,10},{9,11},{10,... | collective-permute-start | bytes 245768 | tf_op jit(solution)/shard_map/ppermute | solution.py:316
  517.3 4.1 collective-permute-start.2
  521.4 56.3 %collective-permute-start.3 = (f32[2,20,128]{2,0,1:T(2,128)S(1)}, f32[2,20,128]{2,0,1:T(2,128)S(1)}, u32[]{:S(2)}, u32[]{:S(2)}) collective-permute-start(f32[2,20,128]{2,0,1:T(2,128)S(1)} %bitcast.42), channel_id=1, source_target_pairs={{0,8},{1,9},{2,10},{3,11},{4,12},{5,13},{6,14},{7,15},{8,0},{9,1},... | collective-permute-start | bytes 61448 | tf_op jit(solution)/shard_map/ppermute | solution.py:316
  577.8 38.1 %collective-permute-start.4 = (f32[1,20,128]{2,0,1:T(1,128)S(1)}, f32[1,20,128]{2,0,1:T(1,128)S(1)}, u32[]{:S(2)}, u32[]{:S(2)}) collective-permute-start(f32[1,20,128]{2,0,1:T(1,128)S(1)} %constant_dynamic-slice_fusion), channel_id=1, source_target_pairs={{0,16},{1,17},{2,18},{3,19},{4,20},{5,21},{6,22},{7,23},{8,24},{9,... | collective-permute-start | bytes 30728 | tf_op jit(solution)/shard_map/ppermute | solution.py:316
  616.6 15.2 %copy-start.1 = (f32[16,16]{1,0:T(8,128)S(1)}, f32[16,16]{1,0:T(8,128)}, u32[]{:S(2)}) copy-start(f32[16,16]{1,0:T(8,128)} %param.24) | copy-start | bytes 3076

commit v3 on v2

--- a/solution.py
+++ b/solution.py
@@ -26,109 +26,147 @@
     return max(d for d in range(1, most + 1) if number % d == 0)
 
 
-def gather_waves(pair_table, fourier, devices, local_pairs, first, count, padded):
+def row_groups(rows):
+    return [(at, min(8, rows - at)) for at in range(0, rows, 8)]
+
+
+def gather_waves(pair_table, fourier, devices, local_pairs, first, count):
     rows = fourier.shape[0]
-    per_read = divisor_up_to(rows, 8)
-    reads = rows // per_read
-    per_write = divisor_up_to(devices, 4)
-
-    def body(table, rows_ref, out_ref, held):
-        step = pl.program_id(0)
-
-        if padded > rows:
-
-            @pl.when(step == 0)
-            def _():
-                held[rows * PITCH :, :] = jnp.zeros(((padded - rows) * PITCH, COLS), F32)
-
-        @pl.when(step < reads)
-        def _():
-            for r in range(per_read):
-                start = pl.multiple_of((step * per_read + r) * PITCH, 8)
-                held[pl.ds(start, WAVES), :] = rows_ref[r].astype(F32)
-
-        @pl.when(step >= reads)
-        def _():
-            def one_device(d, carry):
+    spans = row_groups(rows)
+    groups = len(spans)
+
+    def body(table, rows_ref, out_ref, read, held, written, read_sem, write_sem):
+        reads = [
+            pltpu.make_async_copy(rows_ref.at[pl.ds(at, size)], read.at[pl.ds(at, size)], read_sem.at[g])
+            for g, (at, size) in enumerate(spans)
+        ]
+        writes = [
+            pltpu.make_async_copy(written.at[g], out_ref.at[:, :, g], write_sem.at[g])
+            for g in range(groups)
+        ]
+        for copy in reads:
+            copy.start()
+        if rows % 8:
+            read[rows:] = jnp.zeros((groups * 8 - rows, WAVES, COLS), BF16)
+
+        for g in range(groups):
+            reads[g].wait()
+
+            def widen(r, carry, g=g):
+                held[pl.ds(pl.multiple_of(r * PITCH, 8), WAVES), :] = read[g * 8 + r].astype(F32)
+                return carry
+
+            lax.fori_loop(0, 8, widen, 0)
+
+            def one_device(d, carry, g=g):
                 for s in range(count):
-                    wave = table[((step - reads) * per_write + d) * local_pairs + first + s]
+                    wave = table[d * local_pairs + first + s]
                     both = jnp.concatenate(
                         [
-                            held[pl.ds(wave, padded, stride=PITCH), :],
-                            held[pl.ds(TRUNC - wave, padded, stride=PITCH), :],
+                            held[pl.ds(wave, 8, stride=PITCH), :],
+                            held[pl.ds(TRUNC - wave, 8, stride=PITCH), :],
                         ],
                         axis=0,
                     )
-                    out_ref[d, pl.ds(s * 2 * padded, 2 * padded), :] = both.astype(BF16)
+                    written[g, d, s] = both.astype(BF16)
                 return carry
 
-            lax.fori_loop(0, per_write, one_device, 0)
+            lax.fori_loop(0, devices, one_device, 0)
+            writes[g].start()
+        for copy in writes:
+            copy.wait()
 
     return pl.pallas_call(
         body,
         grid_spec=pltpu.PrefetchScalarGridSpec(
             num_scalar_prefetch=1,
-            grid=(reads + devices // per_write,),
-            in_specs=[
-                pl.BlockSpec((per_read, WAVES, COLS), lambda i, t: (jnp.minimum(i, reads - 1), 0, 0))
-            ],
-            out_specs=pl.BlockSpec(
-                (per_write, count * 2 * padded, COLS), lambda i, t: (jnp.maximum(i - reads, 0), 0, 0)
-            ),
-            scratch_shapes=[pltpu.VMEM((padded * PITCH, COLS), F32)],
+            grid=(1,),
+            in_specs=[pl.BlockSpec(memory_space=pl.ANY)],
+            out_specs=pl.BlockSpec(memory_space=pl.ANY),
+            scratch_shapes=[
+                pltpu.VMEM((groups * 8, WAVES, COLS), BF16),
+                pltpu.VMEM((8 * PITCH, COLS), F32),
+                pltpu.VMEM((groups, devices, count, 16, COLS), BF16),
+                pltpu.SemaphoreType.DMA((groups,)),
+                pltpu.SemaphoreType.DMA((groups,)),
+            ],
         ),
-        out_shape=jax.ShapeDtypeStruct((devices, count * 2 * padded, COLS), BF16),
+        out_shape=jax.ShapeDtypeStruct((devices, count, groups, 16, COLS), BF16),
         compiler_params=pltpu.CompilerParams(vmem_limit_bytes=VMEM),
         cost_estimate=pl.CostEstimate(flops=0, bytes_accessed=20_000_000, transcendentals=0),
         name="gather_waves",
     )(pair_table, fourier)
 
 
-def scatter_waves(pair_table, chunks, spans, rows, devices, local_pairs, padded):
-    per_read = divisor_up_to(devices, 4)
-    reads = devices // per_read
-    per_write = divisor_up_to(rows, 8)
-    writes = rows // per_write
+def scatter_waves(pair_table, chunks, rows, local_pairs):
+    devices = chunks[0].shape[0]
+    spans = row_groups(rows)
+    groups = len(spans)
+    counts = [chunk.shape[1] for chunk in chunks]
 
     def body(table, *refs):
-        chunk_refs, out_ref, held = refs[: len(chunks)], refs[-2], refs[-1]
-        step = pl.program_id(0)
-
-        @pl.when(step < reads)
-        def _():
-            for (first, count), chunk_ref in zip(spans, chunk_refs):
-
-                def one_device(d, carry, first=first, count=count, chunk_ref=chunk_ref):
+        chunk_refs = refs[: len(chunks)]
+        out_ref = refs[len(chunks)]
+        parts = refs[len(chunks) + 1 : 2 * len(chunks) + 1]
+        held, written, read_sem, write_sem = refs[2 * len(chunks) + 1 :]
+        reads = [
+            [
+                pltpu.make_async_copy(chunk.at[:, :, g], part.at[g], read_sem.at[g, c])
+                for c, (chunk, part) in enumerate(zip(chunk_refs, parts))
+            ]
+            for g in range(groups)
+        ]
+        writes = [
+            pltpu.make_async_copy(
+                written.at[g, pl.ds(0, size)], out_ref.at[pl.ds(at, size)], write_sem.at[g]
+            )
+            for g, (at, size) in enumerate(spans)
+        ]
+        for group in reads:
+            for copy in group:
+                copy.start()
+
+        for g in range(groups):
+            for copy in reads[g]:
+                copy.wait()
+
+            def one_device(d, carry, g=g):
+                slot = 0
+                for part, count in zip(parts, counts):
                     for s in range(count):
-                        wave = table[(step * per_read + d) * local_pairs + first + s]
-                        both = chunk_ref[d, pl.ds(s * 2 * padded, 2 * padded), :].astype(F32)
-                        held[pl.ds(wave, padded, stride=PITCH), :] = both[:padded]
-                        held[pl.ds(TRUNC - wave, padded, stride=PITCH), :] = both[padded:]
-                    return carry
-
-                lax.fori_loop(0, per_read, one_device, 0)
-
-        @pl.when(step >= reads)
-        def _():
-            for r in range(per_write):
-                start = pl.multiple_of(((step - reads) * per_write + r) * PITCH, 8)
-                out_ref[r] = held[pl.ds(start, WAVES), :].astype(BF16)
+                        wave = table[d * local_pairs + slot]
+                        both = part[g, d, s].astype(F32)
+                        held[pl.ds(wave, 8, stride=PITCH), :] = both[:8]
+                        held[pl.ds(TRUNC - wave, 8, stride=PITCH), :] = both[8:]
+                        slot += 1
+                return carry
+
+            lax.fori_loop(0, devices, one_device, 0)
+
+            def narrow(r, carry, g=g):
+                row = held[pl.ds(pl.multiple_of(r * PITCH, 8), WAVES), :]
+                written[g, r] = row.astype(BF16)
+                return carry
+
+            lax.fori_loop(0, 8, narrow, 0)
+            writes[g].start()
+        for copy in writes:
+            copy.wait()
 
     return pl.pallas_call(
         body,
         grid_spec=pltpu.PrefetchScalarGridSpec(
             num_scalar_prefetch=1,
-            grid=(reads + writes,),
-            in_specs=[
-                pl.BlockSpec(
-                    (per_read, count * 2 * padded, COLS), lambda i, t: (jnp.minimum(i, reads - 1), 0, 0)
-                )
-                for _, count in spans
-            ],
-            out_specs=pl.BlockSpec(
-                (per_write, WAVES, COLS), lambda i, t: (jnp.maximum(i - reads, 0), 0, 0)
-            ),
-            scratch_shapes=[pltpu.VMEM((padded * PITCH, COLS), F32)],
+            grid=(1,),
+            in_specs=[pl.BlockSpec(memory_space=pl.ANY)] * len(chunks),
+            out_specs=pl.BlockSpec(memory_space=pl.ANY),
+            scratch_shapes=[pltpu.VMEM((groups, devices, count, 16, COLS), BF16) for count in counts]
+            + [
+                pltpu.VMEM((8 * PITCH, COLS), F32),
+                pltpu.VMEM((groups, 8, WAVES, COLS), BF16),
+                pltpu.SemaphoreType.DMA((groups, len(chunks))),
+                pltpu.SemaphoreType.DMA((groups,)),
+            ],
         ),
         out_shape=jax.ShapeDtypeStruct((rows, WAVES, COLS), BF16),
         compiler_params=pltpu.CompilerParams(vmem_limit_bytes=VMEM),
@@ -137,9 +175,9 @@
     )(pair_table, *chunks)
 
 
-def transform(orders, arrived, legendre, fold, unfold, weight, first_map, second_map, depth, damping, first, count, padded):
-    devices = arrived.shape[0]
-    all_rows = devices * padded
+def transform(orders, arrived, legendre, fold, unfold, weight, first_map, second_map, depth, damping, first):
+    devices, count, groups = arrived.shape[:3]
+    all_rows = devices * groups * 8
 
     def body(
         orders_ref, arrived_ref, legendre_ref, fold_ref, unfold_ref, weight_ref, map1_ref, map2_ref, depth_ref,
@@ -156,9 +194,9 @@
 
         tail[0:1, :] = legendre_ref[0, NPACK - 1 : NPACK, :]
 
-        arrived_rows = arrived_ref[...].astype(F32)
-        rows_in[:, :COLS] = arrived_rows[:, :padded].reshape(all_rows, COLS).astype(BF16)
-        rows_in[:, COLS:] = arrived_rows[:, padded:].reshape(all_rows, COLS).astype(BF16)
+        arrived_rows = arrived_ref[...].astype(F32).reshape(devices * groups, 16, COLS)
+        rows_in[:, :COLS] = arrived_rows[:, :8].reshape(all_rows, COLS).astype(BF16)
+        rows_in[:, COLS:] = arrived_rows[:, 8:].reshape(all_rows, COLS).astype(BF16)
 
         def fold_tile(i, carry):
             at = pl.multiple_of(i * 128, 128)
@@ -241,13 +279,14 @@
         lax.fori_loop(0, NHALF // 128, synthesis_tile, 0)
 
         back = jnp.dot(unfold_ref[...], halves[...], preferred_element_type=F32)
-        out_ref[...] = jnp.concatenate(
+        both = jnp.concatenate(
             [
-                back[:, :COLS].reshape(devices, padded, COLS),
-                back[:, COLS:].reshape(devices, padded, COLS),
+                back[:, :COLS].reshape(devices * groups, 8, COLS),
+                back[:, COLS:].reshape(devices * groups, 8, COLS),
             ],
             axis=1,
-        ).astype(BF16)
+        )
+        out_ref[...] = both.astype(BF16).reshape(devices, 1, groups, 16, COLS)
 
     whole = lambda shape: pl.BlockSpec(shape, lambda i, t: (0,) * len(shape))
     return pl.pallas_call(
@@ -256,7 +295,7 @@
             num_scalar_prefetch=1,
             grid=(count,),
             in_specs=[
-                pl.BlockSpec((devices, 2 * padded, COLS), lambda i, t: (0, i, 0)),
+                pl.BlockSpec((devices, 1, groups, 16, COLS), lambda i, t: (0, i, 0, 0, 0)),
                 pl.BlockSpec((1, NPACK, NHALF), lambda i, t: (first + i, 0, 0)),
                 whole(fold.shape),
                 whole(unfold.shape),
@@ -267,7 +306,7 @@
                 whole(damping.shape),
             ],
             out_specs=[
-                pl.BlockSpec((devices, 2 * padded, COLS), lambda i, t: (0, i, 0)),
+                pl.BlockSpec((devices, 1, groups, 16, COLS), lambda i, t: (0, i, 0, 0, 0)),
                 whole((2 * WAVES, COLS)),
                 whole((WAVES + NTAIL, COLS)),
             ],
@@ -316,6 +355,11 @@
         sums = kept + lax.ppermute(sent, AXES, [(d, d ^ bit) for d in range(devices)])
         bit *= 2
     return sums.reshape(rows, columns)
+
+
+def exchange(block):
+    flat = block.reshape(block.shape[0], -1, COLS)
+    return lax.all_to_all(flat, AXES, 0, 0, tiled=True).reshape(block.shape)
 
 
 def on_device(
@@ -362,21 +406,21 @@
     damping = jnp.tile(diffusion.reshape(1, -1), (1, 2))
 
     outgoing = [
-        gather_waves(pair_table, fourier, devices, local_pairs, first, count, padded)
+        gather_waves(pair_table, fourier, devices, local_pairs, first, count)
         for first, count in spans
     ]
-    arrived = [lax.all_to_all(block, AXES, 0, 0, tiled=True) for block in outgoing]
+    arrived = [exchange(block) for block in outgoing]
     done = [
         transform(
             own, block, legendre, fold, unfold, gauss_weight.reshape(NHALF, 1), first_map, second_map,
-            depth, damping, first, count, padded,
+            depth, damping, first,
         )
-        for block, (first, count) in zip(arrived, spans)
+        for block, (first, _) in zip(arrived, spans)
     ]
     energy = sum(low[:WAVES] + high[1 : WAVES + 1] for _, low, high in done)
     spectrum = scatter_sum(energy[:, : COLS // 2] + energy[:, COLS // 2 :], devices)
-    back = [lax.all_to_all(block, AXES, 0, 0, tiled=True) for block, _, _ in done]
-    fourier_out = scatter_waves(pair_table, back, spans, rows, devices, local_pairs, padded)
+    back = [exchange(block) for block, _, _ in done]
+    fourier_out = scatter_waves(pair_table, back, rows, local_pairs)
     return (fourier_out, spectrum)
 
 

time: 632 us -> 625 us (0.989)
  Pallas kernels: 296 us -> 285 us
where the time goes in v3:
time: 625 us
  waiting for transfers between devices  297 us (48%)
  Pallas kernels  285 us (46%)
  starting transfers between devices  26 us (4%)
  other arithmetic  9.23 us (1%)
    pallas_call x2, Pallas kernels, transform(): pl.pallas_call(body, grid_spec=pltpu.PrefetchScalarGridSpec(num_scalar_pr...  254 us
    all_to_all x4, waiting for transfers between devices, exchange(): return lax.all_to_all(flat, AXES, 0, 0, tiled=True).reshape(block.shape)  161 us
    ppermute x5, waiting for transfers between devices, scatter_sum(): lax.ppermute(sent, AXES, [(d, d ^ bit) for d in range(devices)])  136 us
    pallas_call x2, Pallas kernels, gather_waves(): pl.pallas_call(body, grid_spec=pltpu.PrefetchScalarGridSpec(num_scalar_pr...  20.3 us
    all_to_all x4, starting transfers between devices, exchange(): return lax.all_to_all(flat, AXES, 0, 0, tiled=True).reshape(block.shape)  18.6 us
  transfers between devices with their start and end apart: 9, of which 8 were waited for; matrix products, arithmetic and copies ran while one was open for 2% of the time, Pallas kernels for 42%

profile of v3, /device:TPU:0, one launch (start us, length us, event | category | flops | bytes accessed | tf_op | source)
XLA Modules:
  0.0 624.6 jit_solution(16526069918422280096)
XLA Ops:
  0.6 10.2 %gather_waves.2 = bf16[32,10,5,16,128]{4,3,2,1,0:T(8,128)(2,1)} custom-call(s32[640]{0:T(1024)} %table.5, bf16[40,1280,128]{2,1,0:T(8,128)(2,1)} %rows_ref.3), custom_call_target="tpu_custom_call" | custom-call | bytes 20000000 | tf_op jit(solution)/shard_map/gather_waves/pallas_call | solution.py:79
  10.8 7.4 %all-to-all-start = ((bf16[32,800,128]{2,1,0:T(8,128)(2,1)}), bf16[32,800,128]{2,1,0:T(8,128)(2,1)}, u32[]{:S(2)}, u32[]{:S(2)}) async-start(bf16[32,800,128]{2,1,0:T(8,128)(2,1)} %bitcast.39), calls=%async_computation | async-start | bytes 13107200 | tf_op jit(solution)/shard_map/all_to_all | solution.py:362
  18.3 10.2 %gather_waves.3 = bf16[32,10,5,16,128]{4,3,2,1,0:T(8,128)(2,1)} custom-call(s32[640]{0:T(1024)} %table.5, bf16[40,1280,128]{2,1,0:T(8,128)(2,1)} %rows_ref.3), custom_call_target="tpu_custom_call" | custom-call | bytes 20000000 | tf_op jit(solution)/shard_map/gather_waves/pallas_call | solution.py:79
  28.4 135.7 %all-to-all-done = bf16[32,800,128]{2,1,0:T(8,128)(2,1)} async-done(((bf16[32,800,128]{2,1,0:T(8,128)(2,1)}), bf16[32,800,128]{2,1,0:T(8,128)(2,1)}, u32[]{:S(2)}, u32[]{:S(2)}) %all-to-all-start) | async-done | bytes 6553632 | tf_op jit(solution)/shard_map/all_to_all | solution.py:362
  164.1 3.8 all-to-all-start.2
  167.9 1.3 dynamic_slice.34.orders_ref
  175.7 1.9 pad_maximum_fusion.fold_ref
  177.6 2.4 add_convert_fusion.unfold_ref
  180.1 127.0 %transform.2 = (bf16[32,10,5,16,128]{4,3,2,1,0:T(8,128)(2,1)}, f32[2560,128]{1,0:T(8,128)}, f32[1296,128]{1,0:T(8,128)}) custom-call(s32[20]{0:T(128)} %dynamic_slice.34.orders_ref, bf16[32,10,5,16,128]{4,3,2,1,0:T(8,128)(2,1)} %bitcast.1.arrived_ref, bf16[20,1281,640]{2,1,0:T(8,128)(2,1)} %legendre_ref.3, bf16[1280,1280]{1,0:T(8,128)(2,1)} %pad_maximum_fusion.fold_ref, ...), custom_call_target="tpu_custom_call" | custom-call | flops 35000000512 | bytes 30000000 | tf_op jit(solution)/shard_map/transform/pallas_call | solution.py:292
  307.0 6.6 %all-to-all-done.2 = bf16[32,800,128]{2,1,0:T(8,128)(2,1)} async-done(((bf16[32,800,128]{2,1,0:T(8,128)(2,1)}), bf16[32,800,128]{2,1,0:T(8,128)(2,1)}, u32[]{:S(2)}, u32[]{:S(2)}) %all-to-all-start.2) | async-done | bytes 6553632 | tf_op jit(solution)/shard_map/all_to_all | solution.py:362
  313.6 3.6 all-to-all-start.1
  317.3 127.0 %transform.3 = (bf16[32,10,5,16,128]{4,3,2,1,0:T(8,128)(2,1)}, f32[2560,128]{1,0:T(8,128)}, f32[1296,128]{1,0:T(8,128)}) custom-call(s32[20]{0:T(128)} %dynamic_slice.34.orders_ref, bf16[32,10,5,16,128]{4,3,2,1,0:T(8,128)(2,1)} %bitcast.11.arrived_ref, bf16[20,1281,640]{2,1,0:T(8,128)(2,1)} %legendre_ref.3, bf16[1280,1280]{1,0:T(8,128)(2,1)} %pad_maximum_fusion.fold_ref, ...), custom_call_target="tpu_custom_call" | custom-call | flops 35000000512 | bytes 30000000 | tf_op jit(solution)/shard_map/transform/pallas_call | solution.py:292
  444.3 18.7 %all-to-all-done.1 = bf16[32,800,128]{2,1,0:T(8,128)(2,1)} async-done(((bf16[32,800,128]{2,1,0:T(8,128)(2,1)}), bf16[32,800,128]{2,1,0:T(8,128)(2,1)}, u32[]{:S(2)}, u32[]{:S(2)}) %all-to-all-start.1) | async-done | bytes 6553632 | tf_op jit(solution)/shard_map/all_to_all | solution.py:362
  463.0 3.8 all-to-all-start.3
  466.9 1.3 add_add_fusion
  468.8 1.3 collective-permute-done
  470.3 1.6 collective-permute-start.1
  472.0 42.3 %collective-permute-done.1 = f32[8,20,128]{2,0,1:T(8,128)S(1)} collective-permute-done((f32[8,20,128]{2,0,1:T(8,128)S(1)}, f32[8,20,128]{2,0,1:T(8,128)S(1)}, u32[]{:S(2)}, u32[]{:S(2)}) %collective-permute-start.1) | collective-permute-done | bytes 81952 | tf_op jit(solution)/shard_map/ppermute | solution.py:355
  514.5 4.0 collective-permute-done.2
  518.5 1.4 collective-permute-start.3
  520.0 54.9 %collective-permute-done.3 = f32[2,20,128]{2,0,1:T(2,128)S(1)} collective-permute-done((f32[2,20,128]{2,0,1:T(2,128)S(1)}, f32[2,20,128]{2,0,1:T(2,128)S(1)}, u32[]{:S(2)}, u32[]{:S(2)}) %collective-permute-start.3) | collective-permute-done | bytes 20512 | tf_op jit(solution)/shard_map/ppermute | solution.py:355
  574.9 4.1 collective-permute-start.4
  579.0 34.0 %collective-permute-done.4 = f32[1,20,128]{2,0,1:T(1,128)S(1)} collective-permute-done((f32[1,20,128]{2,0,1:T(1,128)S(1)}, f32[1,20,128]{2,0,1:T(1,128)S(1)}, u32[]{:S(2)}, u32[]{:S(2)}) %collective-permute-start.4) | collective-permute-done | bytes 10272 | tf_op jit(solution)/shard_map/ppermute | solution.py:355
  613.7 10.9 %scatter_waves.1 = bf16[40,1280,128]{2,1,0:T(8,128)(2,1)} custom-call(s32[640]{0:T(1024)} %table.5, bf16[32,10,5,16,128]{4,3,2,1,0:T(8,128)(2,1)} %bitcast.9.refs_0_, bf16[32,10,5,16,128]{4,3,2,1,0:T(8,128)(2,1)} %bitcast.13.refs_1_), custom_call_target="tpu_custom_call" | custom-call | bytes 26000000 | tf_op jit(solution)/shard_map/scatter_waves/pallas_call | solution.py:156
  (61 shorter events, 8.2 us)
Async XLA Ops:
  0.6 169.4 %copy-start = (f32[16,16]{1,0:T(8,128)S(1)}, f32[16,16]{1,0:T(8,128)}, u32[]{:S(2)}) copy-start(f32[16,16]{1,0:T(8,128)} %param.24) | copy-start | bytes 3076
  10.8 153.3 %all-to-all-start = ((bf16[32,800,128]{2,1,0:T(8,128)(2,1)}), bf16[32,800,128]{2,1,0:T(8,128)(2,1)}, u32[]{:S(2)}, u32[]{:S(2)}) async-start(bf16[32,800,128]{2,1,0:T(8,128)(2,1)} %bitcast.39), calls=%async_computation | async-start | bytes 13107200 | tf_op jit(solution)/shard_map/all_to_all | solution.py:362
  164.1 5.1 copy-start.7
  164.1 6.0 copy-start.5
  164.1 6.9 %copy-start.9 = (f32[16]{0:T(128)S(1)}, f32[16]{0:T(128)}, u32[]{:S(2)}) copy-start(f32[16]{0:T(128)} %param.26) | copy-start | bytes 196
  164.1 7.6 %copy-start.8 = (f32[4,16]{1,0:T(4,128)S(1)}, f32[4,16]{1,0:T(4,128)}, u32[]{:S(2)}) copy-start(f32[4,16]{1,0:T(4,128)} %param.27) | copy-start | bytes 772
  164.1 9.8 %copy-start.6 = (s32[1280]{0:T(1024)S(1)}, s32[1280]{0:T(1024)}, u32[]{:S(2)}) copy-start(s32[1280]{0:T(1024)} %param.22) | copy-start | bytes 15364
  164.1 149.5 %all-to-all-start.2 = ((bf16[32,800,128]{2,1,0:T(8,128)(2,1)}), bf16[32,800,128]{2,1,0:T(8,128)(2,1)}, u32[]{:S(2)}, u32[]{:S(2)}) async-start(bf16[32,800,128]{2,1,0:T(8,128)(2,1)} %bitcast.38), calls=%async_computation.2 | async-start | bytes 13107200 | tf_op jit(solution)/shard_map/all_to_all | solution.py:362
  313.6 149.4 %all-to-all-start.1 = ((bf16[32,800,128]{2,1,0:T(8,128)(2,1)}), bf16[32,800,128]{2,1,0:T(8,128)(2,1)}, u32[]{:S(2)}, u32[]{:S(2)}) async-start(bf16[32,800,128]{2,1,0:T(8,128)(2,1)} %bitcast.41), calls=%async_computation.1 | async-start | bytes 13107200 | tf_op jit(solution)/shard_map/all_to_all | solution.py:362
  463.0 3.8 copy-start.2
  463.0 3.8 copy-start.3
  463.0 3.8 copy-start.4
  463.0 150.6 %all-to-all-start.3 = ((bf16[32,800,128]{2,1,0:T(8,128)(2,1)}), bf16[32,800,128]{2,1,0:T(8,128)(2,1)}, u32[]{:S(2)}, u32[]{:S(2)}) async-start(bf16[32,800,128]{2,1,0:T(8,128)(2,1)} %bitcast.40), calls=%async_computation.3 | async-start | bytes 13107200 | tf_op jit(solution)/shard_map/all_to_all | solution.py:362
  468.7 1.5 collective-permute-start
  470.3 44.0 %collective-permute-start.1 = (f32[8,20,128]{2,0,1:T(8,128)S(1)}, f32[8,20,128]{2,0,1:T(8,128)S(1)}, u32[]{:S(2)}, u32[]{:S(2)}) collective-permute-start(f32[8,20,128]{2,0,1:T(8,128)S(1)} %bitcast.50), channel_id=1, source_target_pairs={{0,2},{1,3},{2,0},{3,1},{4,6},{5,7},{6,4},{7,5},{8,10},{9,11},{10,... | collective-permute-start | bytes 245768 | tf_op jit(solution)/shard_map/ppermute | solution.py:355
  514.4 4.1 collective-permute-start.2
  518.5 56.3 %collective-permute-start.3 = (f32[2,20,128]{2,0,1:T(2,128)S(1)}, f32[2,20,128]{2,0,1:T(2,128)S(1)}, u32[]{:S(2)}, u32[]{:S(2)}) collective-permute-start(f32[2,20,128]{2,0,1:T(2,128)S(1)} %bitcast.54), channel_id=1, source_target_pairs={{0,8},{1,9},{2,10},{3,11},{4,12},{5,13},{6,14},{7,15},{8,0},{9,1},... | collective-permute-start | bytes 61448 | tf_op jit(solution)/shard_map/ppermute | solution.py:355
  574.9 38.1 %collective-permute-start.4 = (f32[1,20,128]{2,0,1:T(1,128)S(1)}, f32[1,20,128]{2,0,1:T(1,128)S(1)}, u32[]{:S(2)}, u32[]{:S(2)}) collective-permute-start(f32[1,20,128]{2,0,1:T(1,128)S(1)} %constant_dynamic-slice_fusion), channel_id=1, source_target_pairs={{0,16},{1,17},{2,18},{3,19},{4,20},{5,21},{6,22},{7,23},{8,24},{9,... | collective-permute-start | bytes 30728 | tf_op jit(solution)/shard_map/ppermute | solution.py:355
  613.7 10.9 %copy-start.1 = (f32[16,16]{1,0:T(8,128)S(1)}, f32[16,16]{1,0:T(8,128)}, u32[]{:S(2)}) copy-start(f32[16,16]{1,0:T(8,128)} %param.24) | copy-start | bytes 3076

commit v4 on v3

--- a/solution.py
+++ b/solution.py
@@ -85,7 +85,7 @@
             out_specs=pl.BlockSpec(memory_space=pl.ANY),
             scratch_shapes=[
                 pltpu.VMEM((groups * 8, WAVES, COLS), BF16),
-                pltpu.VMEM((8 * PITCH, COLS), F32),
+                pltpu.VMEM((9 * PITCH, COLS), F32),
                 pltpu.VMEM((groups, devices, count, 16, COLS), BF16),
                 pltpu.SemaphoreType.DMA((groups,)),
                 pltpu.SemaphoreType.DMA((groups,)),
@@ -162,7 +162,7 @@
             out_specs=pl.BlockSpec(memory_space=pl.ANY),
             scratch_shapes=[pltpu.VMEM((groups, devices, count, 16, COLS), BF16) for count in counts]
             + [
-                pltpu.VMEM((8 * PITCH, COLS), F32),
+                pltpu.VMEM((9 * PITCH, COLS), F32),
                 pltpu.VMEM((groups, 8, WAVES, COLS), BF16),
                 pltpu.SemaphoreType.DMA((groups, len(chunks))),
                 pltpu.SemaphoreType.DMA((groups,)),
@@ -344,17 +344,17 @@
 
 def scatter_sum(parts, devices):
     device = lax.axis_index(AXES)
-    rows, columns = parts.shape[0] // devices, parts.shape[1]
-    sums = parts.reshape(devices, rows * columns // COLS, COLS)
+    sums = parts.reshape(devices, -1, COLS)
     bit = 1
     while bit < devices:
         sums = sums.reshape((sums.shape[0] // 2, 2) + sums.shape[1:])
         own = (device // bit) % 2
         kept = lax.dynamic_index_in_dim(sums, own, 1, keepdims=False)
         sent = lax.dynamic_index_in_dim(sums, 1 - own, 1, keepdims=False)
-        sums = kept + lax.ppermute(sent, AXES, [(d, d ^ bit) for d in range(devices)])
+        came = lax.ppermute(sent, AXES, [(d, d ^ bit) for d in range(devices)])
+        sums = kept + came
         bit *= 2
-    return sums.reshape(rows, columns)
+    return kept, came
 
 
 def exchange(block):
@@ -418,9 +418,11 @@
         for block, (first, _) in zip(arrived, spans)
     ]
     energy = sum(low[:WAVES] + high[1 : WAVES + 1] for _, low, high in done)
-    spectrum = scatter_sum(energy[:, : COLS // 2] + energy[:, COLS // 2 :], devices)
+    halves = scatter_sum(energy[:, : COLS // 2] + energy[:, COLS // 2 :], devices)
     back = [exchange(block) for block, _, _ in done]
     fourier_out = scatter_waves(pair_table, back, rows, local_pairs)
+    fourier_out, *halves = lax.optimization_barrier((fourier_out, *halves))
+    spectrum = (halves[0] + halves[1]).reshape(NLAT // devices, FIELDS * LEVELS)
     return (fourier_out, spectrum)
 
 

time: 625 us -> 625 us (level)
    all_to_all x4, waiting for transfers between devices: 161 us -> 195 us  [exchange(): return lax.all_to_all(flat, AXES, 0, 0, tiled=True).reshape(block.shape)]
    ppermute x5, waiting for transfers between devices: 136 us -> 103 us  [scatter_sum(): came = lax.ppermute(sent, AXES, [(d, d ^ bit) for d in range(devices)])]
  transfers between devices with their start and end apart: 9 -> 9, of which waited for: 8 -> 8; matrix products, arithmetic and copies ran while one was open for 2% -> 2% of each run, Pallas kernels for 42% -> 44%
where the time goes in v4:
time: 625 us
  waiting for transfers between devices  297 us (48%)
  Pallas kernels  285 us (46%)
  starting transfers between devices  26 us (4%)
  other arithmetic  9.2 us (1%)
    pallas_call x2, Pallas kernels, transform(): pl.pallas_call(body, grid_spec=pltpu.PrefetchScalarGridSpec(num_scalar_pr...  254 us
    all_to_all x4, waiting for transfers between devices, exchange(): return lax.all_to_all(flat, AXES, 0, 0, tiled=True).reshape(block.shape)  195 us
    ppermute x5, waiting for transfers between devices, scatter_sum(): came = lax.ppermute(sent, AXES, [(d, d ^ bit) for d in range(devices)])  103 us
    pallas_call x2, Pallas kernels, gather_waves(): pl.pallas_call(body, grid_spec=pltpu.PrefetchScalarGridSpec(num_scalar_pr...  20.3 us
    all_to_all x4, starting transfers between devices, exchange(): return lax.all_to_all(flat, AXES, 0, 0, tiled=True).reshape(block.shape)  18.6 us
  transfers between devices with their start and end apart: 9, of which 8 were waited for; matrix products, arithmetic and copies ran while one was open for 2% of the time, Pallas kernels for 44%

profile of v4, /device:TPU:0, one launch (start us, length us, event | category | flops | bytes accessed | tf_op | source)
XLA Modules:
  0.0 624.6 jit_solution(16808251895920281786)
XLA Ops:
  0.6 10.2 %gather_waves.2 = bf16[32,10,5,16,128]{4,3,2,1,0:T(8,128)(2,1)} custom-call(s32[640]{0:T(1024)} %table.5, bf16[40,1280,128]{2,1,0:T(8,128)(2,1)} %rows_ref.3), custom_call_target="tpu_custom_call" | custom-call | bytes 20000000 | tf_op jit(solution)/shard_map/gather_waves/pallas_call | solution.py:79
  10.8 7.4 %all-to-all-start = ((bf16[32,800,128]{2,1,0:T(8,128)(2,1)}), bf16[32,800,128]{2,1,0:T(8,128)(2,1)}, u32[]{:S(2)}, u32[]{:S(2)}) async-start(bf16[32,800,128]{2,1,0:T(8,128)(2,1)} %bitcast.39), calls=%async_computation | async-start | bytes 13107200 | tf_op jit(solution)/shard_map/all_to_all | solution.py:362
  18.3 10.1 %gather_waves.3 = bf16[32,10,5,16,128]{4,3,2,1,0:T(8,128)(2,1)} custom-call(s32[640]{0:T(1024)} %table.5, bf16[40,1280,128]{2,1,0:T(8,128)(2,1)} %rows_ref.3), custom_call_target="tpu_custom_call" | custom-call | bytes 20000000 | tf_op jit(solution)/shard_map/gather_waves/pallas_call | solution.py:79
  28.4 135.7 %all-to-all-done = bf16[32,800,128]{2,1,0:T(8,128)(2,1)} async-done(((bf16[32,800,128]{2,1,0:T(8,128)(2,1)}), bf16[32,800,128]{2,1,0:T(8,128)(2,1)}, u32[]{:S(2)}, u32[]{:S(2)}) %all-to-all-start) | async-done | bytes 6553632 | tf_op jit(solution)/shard_map/all_to_all | solution.py:362
  164.1 3.8 all-to-all-start.2
  167.9 1.3 dynamic_slice.34.orders_ref
  175.8 1.9 pad_maximum_fusion.fold_ref
  177.7 2.4 add_convert_fusion.unfold_ref
  180.1 126.9 %transform.2 = (bf16[32,10,5,16,128]{4,3,2,1,0:T(8,128)(2,1)}, f32[2560,128]{1,0:T(8,128)}, f32[1296,128]{1,0:T(8,128)}) custom-call(s32[20]{0:T(128)} %dynamic_slice.34.orders_ref, bf16[32,10,5,16,128]{4,3,2,1,0:T(8,128)(2,1)} %bitcast.1.arrived_ref, bf16[20,1281,640]{2,1,0:T(8,128)(2,1)} %legendre_ref.3, bf16[1280,1280]{1,0:T(8,128)(2,1)} %pad_maximum_fusion.fold_ref, ...), custom_call_target="tpu_custom_call" | custom-call | flops 35000000512 | bytes 30000000 | tf_op jit(solution)/shard_map/transform/pallas_call | solution.py:292
  307.0 6.6 %all-to-all-done.2 = bf16[32,800,128]{2,1,0:T(8,128)(2,1)} async-done(((bf16[32,800,128]{2,1,0:T(8,128)(2,1)}), bf16[32,800,128]{2,1,0:T(8,128)(2,1)}, u32[]{:S(2)}, u32[]{:S(2)}) %all-to-all-start.2) | async-done | bytes 6553632 | tf_op jit(solution)/shard_map/all_to_all | solution.py:362
  313.6 3.6 all-to-all-start.1
  317.3 127.0 %transform.3 = (bf16[32,10,5,16,128]{4,3,2,1,0:T(8,128)(2,1)}, f32[2560,128]{1,0:T(8,128)}, f32[1296,128]{1,0:T(8,128)}) custom-call(s32[20]{0:T(128)} %dynamic_slice.34.orders_ref, bf16[32,10,5,16,128]{4,3,2,1,0:T(8,128)(2,1)} %bitcast.11.arrived_ref, bf16[20,1281,640]{2,1,0:T(8,128)(2,1)} %legendre_ref.3, bf16[1280,1280]{1,0:T(8,128)(2,1)} %pad_maximum_fusion.fold_ref, ...), custom_call_target="tpu_custom_call" | custom-call | flops 35000000512 | bytes 30000000 | tf_op jit(solution)/shard_map/transform/pallas_call | solution.py:292
  444.3 18.7 %all-to-all-done.1 = bf16[32,800,128]{2,1,0:T(8,128)(2,1)} async-done(((bf16[32,800,128]{2,1,0:T(8,128)(2,1)}), bf16[32,800,128]{2,1,0:T(8,128)(2,1)}, u32[]{:S(2)}, u32[]{:S(2)}) %all-to-all-start.1) | async-done | bytes 6553632 | tf_op jit(solution)/shard_map/all_to_all | solution.py:362
  463.0 3.8 all-to-all-start.3
  466.9 1.3 add_add_fusion
  468.8 1.3 collective-permute-done
  470.3 1.6 collective-permute-start.1
  471.9 42.3 %collective-permute-done.1 = f32[8,20,128]{2,0,1:T(8,128)S(1)} collective-permute-done((f32[8,20,128]{2,0,1:T(8,128)S(1)}, f32[8,20,128]{2,0,1:T(8,128)S(1)}, u32[]{:S(2)}, u32[]{:S(2)}) %collective-permute-start.1) | collective-permute-done | bytes 81952 | tf_op jit(solution)/shard_map/ppermute | solution.py:354
  514.5 4.0 collective-permute-done.2
  518.5 1.4 collective-permute-start.3
  520.0 54.9 %collective-permute-done.3 = f32[2,20,128]{2,0,1:T(2,128)S(1)} collective-permute-done((f32[2,20,128]{2,0,1:T(2,128)S(1)}, f32[2,20,128]{2,0,1:T(2,128)S(1)}, u32[]{:S(2)}, u32[]{:S(2)}) %collective-permute-start.3) | collective-permute-done | bytes 20512 | tf_op jit(solution)/shard_map/ppermute | solution.py:354
  574.9 4.1 collective-permute-start.4
  579.0 34.0 %all-to-all-done.3 = bf16[32,800,128]{2,1,0:T(8,128)(2,1)} async-done(((bf16[32,800,128]{2,1,0:T(8,128)(2,1)}), bf16[32,800,128]{2,1,0:T(8,128)(2,1)}, u32[]{:S(2)}, u32[]{:S(2)}) %all-to-all-start.3) | async-done | bytes 6553632 | tf_op jit(solution)/shard_map/all_to_all | solution.py:362
  612.9 10.9 %scatter_waves.1 = bf16[40,1280,128]{2,1,0:T(8,128)(2,1)} custom-call(s32[640]{0:T(1024)} %table.5, bf16[32,10,5,16,128]{4,3,2,1,0:T(8,128)(2,1)} %bitcast.9.refs_0_, bf16[32,10,5,16,128]{4,3,2,1,0:T(8,128)(2,1)} %bitcast.13.refs_1_), custom_call_target="tpu_custom_call" | custom-call | bytes 26000000 | tf_op jit(solution)/shard_map/scatter_waves/pallas_call | solution.py:156
  (61 shorter events, 8.3 us)
Async XLA Ops:
  0.6 169.4 %copy-start = (f32[16,16]{1,0:T(8,128)S(1)}, f32[16,16]{1,0:T(8,128)}, u32[]{:S(2)}) copy-start(f32[16,16]{1,0:T(8,128)} %param.24) | copy-start | bytes 3076
  10.8 153.3 %all-to-all-start = ((bf16[32,800,128]{2,1,0:T(8,128)(2,1)}), bf16[32,800,128]{2,1,0:T(8,128)(2,1)}, u32[]{:S(2)}, u32[]{:S(2)}) async-start(bf16[32,800,128]{2,1,0:T(8,128)(2,1)} %bitcast.39), calls=%async_computation | async-start | bytes 13107200 | tf_op jit(solution)/shard_map/all_to_all | solution.py:362
  164.1 5.1 copy-start.7
  164.1 5.9 copy-start.5
  164.1 6.9 %copy-start.9 = (f32[16]{0:T(128)S(1)}, f32[16]{0:T(128)}, u32[]{:S(2)}) copy-start(f32[16]{0:T(128)} %param.26) | copy-start | bytes 196
  164.1 7.7 %copy-start.8 = (f32[4,16]{1,0:T(4,128)S(1)}, f32[4,16]{1,0:T(4,128)}, u32[]{:S(2)}) copy-start(f32[4,16]{1,0:T(4,128)} %param.27) | copy-start | bytes 772
  164.1 9.9 %copy-start.6 = (s32[1280]{0:T(1024)S(1)}, s32[1280]{0:T(1024)}, u32[]{:S(2)}) copy-start(s32[1280]{0:T(1024)} %param.22) | copy-start | bytes 15364
  164.1 149.5 %all-to-all-start.2 = ((bf16[32,800,128]{2,1,0:T(8,128)(2,1)}), bf16[32,800,128]{2,1,0:T(8,128)(2,1)}, u32[]{:S(2)}, u32[]{:S(2)}) async-start(bf16[32,800,128]{2,1,0:T(8,128)(2,1)} %bitcast.38), calls=%async_computation.2 | async-start | bytes 13107200 | tf_op jit(solution)/shard_map/all_to_all | solution.py:362
  313.6 149.4 %all-to-all-start.1 = ((bf16[32,800,128]{2,1,0:T(8,128)(2,1)}), bf16[32,800,128]{2,1,0:T(8,128)(2,1)}, u32[]{:S(2)}, u32[]{:S(2)}) async-start(bf16[32,800,128]{2,1,0:T(8,128)(2,1)} %bitcast.41), calls=%async_computation.1 | async-start | bytes 13107200 | tf_op jit(solution)/shard_map/all_to_all | solution.py:362
  463.0 3.8 copy-start.2
  463.0 3.8 copy-start.3
  463.0 3.8 copy-start.4
  463.0 149.9 %all-to-all-start.3 = ((bf16[32,800,128]{2,1,0:T(8,128)(2,1)}), bf16[32,800,128]{2,1,0:T(8,128)(2,1)}, u32[]{:S(2)}, u32[]{:S(2)}) async-start(bf16[32,800,128]{2,1,0:T(8,128)(2,1)} %bitcast.40), calls=%async_computation.3 | async-start | bytes 13107200 | tf_op jit(solution)/shard_map/all_to_all | solution.py:362
  468.6 1.5 collective-permute-start
  470.3 44.0 %collective-permute-start.1 = (f32[8,20,128]{2,0,1:T(8,128)S(1)}, f32[8,20,128]{2,0,1:T(8,128)S(1)}, u32[]{:S(2)}, u32[]{:S(2)}) collective-permute-start(f32[8,20,128]{2,0,1:T(8,128)S(1)} %bitcast.50), channel_id=1, source_target_pairs={{0,2},{1,3},{2,0},{3,1},{4,6},{5,7},{6,4},{7,5},{8,10},{9,11},{10,... | collective-permute-start | bytes 245768 | tf_op jit(solution)/shard_map/ppermute | solution.py:354
  514.4 4.1 collective-permute-start.2
  518.5 56.3 %collective-permute-start.3 = (f32[2,20,128]{2,0,1:T(2,128)S(1)}, f32[2,20,128]{2,0,1:T(2,128)S(1)}, u32[]{:S(2)}, u32[]{:S(2)}) collective-permute-start(f32[2,20,128]{2,0,1:T(2,128)S(1)} %bitcast.54), channel_id=1, source_target_pairs={{0,8},{1,9},{2,10},{3,11},{4,12},{5,13},{6,14},{7,15},{8,0},{9,1},... | collective-permute-start | bytes 61448 | tf_op jit(solution)/shard_map/ppermute | solution.py:354
  574.9 48.9 %collective-permute-start.4 = (f32[1,20,128]{2,0,1:T(1,128)S(1)}, f32[1,20,128]{2,0,1:T(1,128)S(1)}, u32[]{:S(2)}, u32[]{:S(2)}) collective-permute-start(f32[1,20,128]{2,0,1:T(1,128)S(1)} %get-tuple-element.88), channel_id=1, source_target_pairs={{0,16},{1,17},{2,18},{3,19},{4,20},{5,21},{6,22},{7,23},{8,24},{9,... | collective-permute-start | bytes 30728 | tf_op jit(solution)/shard_map/ppermute | solution.py:354
  612.9 11.6 %copy-start.1 = (f32[16,16]{1,0:T(8,128)S(1)}, f32[16,16]{1,0:T(8,128)}, u32[]{:S(2)}) copy-start(f32[16,16]{1,0:T(8,128)} %param.24) | copy-start | bytes 3076

commit v5 on v4

--- a/solution.py
+++ b/solution.py
@@ -181,7 +181,7 @@
 
     def body(
         orders_ref, arrived_ref, legendre_ref, fold_ref, unfold_ref, weight_ref, map1_ref, map2_ref, depth_ref,
-        damping_ref, out_ref, low_ref, high_ref, rows_in, folded, blocks, halves, tail,
+        damping_ref, out_ref, low_ref, high_ref, rows_in, folded, analysed, blocks, halves, tail,
     ):
         step = pl.program_id(0)
         order = orders_ref[first + step]
@@ -198,23 +198,16 @@
         rows_in[:, :COLS] = arrived_rows[:, :8].reshape(all_rows, COLS).astype(BF16)
         rows_in[:, COLS:] = arrived_rows[:, 8:].reshape(all_rows, COLS).astype(BF16)
 
-        def fold_tile(i, carry):
-            at = pl.multiple_of(i * 128, 128)
-            for part in range(2):
-                sums = jnp.dot(
-                    fold_ref[pl.ds(pl.multiple_of(part * NHALF + at, 128), 128), :],
-                    rows_in[...],
-                    preferred_element_type=F32,
-                )
-                folded[pl.ds(at, 128), part * 256 : part * 256 + 256] = (
-                    weight_ref[pl.ds(at, 128), :] * sums
-                ).astype(BF16)
-            return carry
-
-        lax.fori_loop(0, NHALF // 128, fold_tile, 0)
-
-        def update(start, slab, size):
-            gathered = jnp.dot(slab, folded[...], preferred_element_type=F32)
+        folds = weight_ref[...] * jnp.dot(fold_ref[...], rows_in[...], preferred_element_type=F32)
+        folded[:, :256] = folds[:NHALF].astype(BF16)
+        folded[:, 256:] = folds[NHALF:].astype(BF16)
+        analysed[: NPACK - 1, :] = jnp.dot(
+            legendre_ref[0, : NPACK - 1, :], folded[...], preferred_element_type=F32
+        )
+        analysed[NPACK - 1 :, :] = jnp.dot(tail[...], folded[...], preferred_element_type=F32)
+
+        def update(start, size):
+            gathered = analysed[pl.ds(start, size), :]
             packed = lax.broadcasted_iota(jnp.int32, (size, COLS), 0) + start
             in_first = packed <= TRUNC - order
             odd = jnp.where(in_first, packed, packed + order) % 2 == 1
@@ -250,33 +243,23 @@
 
         def update_tile(i, carry):
             start = pl.multiple_of(i * KTILE, KTILE)
-            low = update(start, legendre_ref[0, pl.ds(start, KTILE), :], KTILE)
+            low = update(start, KTILE)
             low_ref[pl.ds(start + order, KTILE), :] += low
             return carry
 
         lax.fori_loop(0, (NPACK - 1) // KTILE, update_tile, 0)
-        update(NPACK - 1, tail[...], NTAIL)
-
-        def synthesis_tile(i, carry):
-            at = pl.multiple_of(i * 128, 128)
-            both = lax.dot_general(
-                legendre_ref[0, : NPACK - 1, pl.ds(at, 128)],
-                blocks[: NPACK - 1, :],
-                (((0,), (0,)), ((), ())),
-                preferred_element_type=F32,
-            ) + lax.dot_general(
-                tail[:, pl.ds(at, 128)],
-                blocks[NPACK - 1 :, :],
-                (((0,), (0,)), ((), ())),
-                preferred_element_type=F32,
-            )
-            halves[pl.ds(at, 128), :] = (both[:, :256] + both[:, 256:]).astype(BF16)
-            halves[pl.ds(pl.multiple_of(NHALF + at, 128), 128), :] = (
-                both[:, :256] - both[:, 256:]
-            ).astype(BF16)
-            return carry
-
-        lax.fori_loop(0, NHALF // 128, synthesis_tile, 0)
+        update(NPACK - 1, NTAIL)
+
+        synthesised = lax.dot_general(
+            legendre_ref[0, : NPACK - 1, :],
+            blocks[: NPACK - 1, :],
+            (((0,), (0,)), ((), ())),
+            preferred_element_type=F32,
+        ) + lax.dot_general(
+            tail[...], blocks[NPACK - 1 :, :], (((0,), (0,)), ((), ())), preferred_element_type=F32
+        )
+        halves[:NHALF, :] = (synthesised[:, :256] + synthesised[:, 256:]).astype(BF16)
+        halves[NHALF:, :] = (synthesised[:, :256] - synthesised[:, 256:]).astype(BF16)
 
         back = jnp.dot(unfold_ref[...], halves[...], preferred_element_type=F32)
         both = jnp.concatenate(
@@ -313,6 +296,7 @@
             scratch_shapes=[
                 pltpu.VMEM((all_rows, 2 * COLS), BF16),
                 pltpu.VMEM((NHALF, 4 * COLS), BF16),
+                pltpu.VMEM((WAVES + NTAIL, 4 * COLS), F32),
                 pltpu.VMEM((WAVES + NTAIL, 4 * COLS), BF16),
                 pltpu.VMEM((NLAT, 2 * COLS), BF16),
                 pltpu.VMEM((NTAIL, NHALF), BF16),
@@ -370,7 +354,7 @@
     local_pairs = legendre.shape[0]
     padded = -(-rows // 8) * 8
     chunks = min(2, local_pairs)
-    cuts = [local_pairs * c // chunks for c in range(chunks + 1)]
+    cuts = [0, -(-local_pairs * 9 // 20), local_pairs][: chunks + 1]
     spans = [(cuts[c], cuts[c + 1] - cuts[c]) for c in range(chunks)]
     own = lax.dynamic_slice_in_dim(
         pair_table, lax.axis_index(AXES) * local_pairs, local_pairs
@@ -412,7 +396,7 @@
     arrived = [exchange(block) for block in outgoing]
     done = [
         transform(
-            own, block, legendre, fold, unfold, gauss_weight.reshape(NHALF, 1), first_map, second_map,
+            own, block, legendre, fold, unfold, jnp.tile(gauss_weight, 2).reshape(2 * NHALF, 1), first_map, second_map,
             depth, damping, first,
         )
         for block, (first, _) in zip(arrived, spans)

time: 625 us -> 625 us (level)
  Pallas kernels: 285 us -> 260 us
  waiting for transfers between devices: 297 us -> 321 us
    pallas_call x2, Pallas kernels: 254 us -> 229 us  [transform(): pl.pallas_call(body, grid_spec=pltpu.PrefetchScalarGridSpec(num_scalar_pr...]
    all_to_all x4, waiting for transfers between devices: 195 us -> 209 us  [exchange(): return lax.all_to_all(flat, AXES, 0, 0, tiled=True).reshape(block.shape)]
    ppermute x5, waiting for transfers between devices: 103 us -> 113 us  [scatter_sum(): came = lax.ppermute(sent, AXES, [(d, d ^ bit) for d in range(devices)])]
  transfers between devices with their start and end apart: 9 -> 9, of which waited for: 8 -> 8; matrix products, arithmetic and copies ran while one was open for 2% -> 2% of each run, Pallas kernels for 44% -> 40%
where the time goes in v5:
time: 625 us; the launch traced here: 624 us
  waiting for transfers between devices  321 us (51%)
  Pallas kernels  260 us (42%)
  starting transfers between devices  26.8 us (4%)
  other arithmetic  9.17 us (1%)
    pallas_call x2, Pallas kernels, transform(): pl.pallas_call(body, grid_spec=pltpu.PrefetchScalarGridSpec(num_scalar_pr...  229 us
    all_to_all x4, waiting for transfers between devices, exchange(): return lax.all_to_all(flat, AXES, 0, 0, tiled=True).reshape(block.shape)  209 us
    ppermute x5, waiting for transfers between devices, scatter_sum(): came = lax.ppermute(sent, AXES, [(d, d ^ bit) for d in range(devices)])  113 us
    pallas_call x2, Pallas kernels, gather_waves(): pl.pallas_call(body, grid_spec=pltpu.PrefetchScalarGridSpec(num_scalar_pr...  20.3 us
    all_to_all x4, starting transfers between devices, exchange(): return lax.all_to_all(flat, AXES, 0, 0, tiled=True).reshape(block.shape)  18.8 us
  transfers between devices with their start and end apart: 9, of which 8 were waited for; matrix products, arithmetic and copies ran while one was open for 2% of the time, Pallas kernels for 40%

profile of v5, /device:TPU:0, one launch (start us, length us, event | category | flops | bytes accessed | tf_op | source)
XLA Modules:
  0.0 624.4 jit_solution(14399247664206595242)
XLA Ops:
  0.6 9.9 %gather_waves.2 = bf16[32,9,5,16,128]{4,3,2,1,0:T(8,128)(2,1)} custom-call(s32[640]{0:T(1024)} %table.5, bf16[40,1280,128]{2,1,0:T(8,128)(2,1)} %rows_ref.3), custom_call_target="tpu_custom_call" | custom-call | bytes 20000000 | tf_op jit(solution)/shard_map/gather_waves/pallas_call | solution.py:79
  10.5 7.4 %all-to-all-start = ((bf16[32,720,128]{2,1,0:T(8,128)(2,1)}), bf16[32,720,128]{2,1,0:T(8,128)(2,1)}, u32[]{:S(2)}, u32[]{:S(2)}) async-start(bf16[32,720,128]{2,1,0:T(8,128)(2,1)} %bitcast.44), calls=%async_computation | async-start | bytes 11796480 | tf_op jit(solution)/shard_map/all_to_all | solution.py:346
  18.0 10.4 %gather_waves.3 = bf16[32,11,5,16,128]{4,3,2,1,0:T(8,128)(2,1)} custom-call(s32[640]{0:T(1024)} %table.5, bf16[40,1280,128]{2,1,0:T(8,128)(2,1)} %rows_ref.3), custom_call_target="tpu_custom_call" | custom-call | bytes 20000000 | tf_op jit(solution)/shard_map/gather_waves/pallas_call | solution.py:79
  28.4 120.9 %all-to-all-done = bf16[32,720,128]{2,1,0:T(8,128)(2,1)} async-done(((bf16[32,720,128]{2,1,0:T(8,128)(2,1)}), bf16[32,720,128]{2,1,0:T(8,128)(2,1)}, u32[]{:S(2)}, u32[]{:S(2)}) %all-to-all-start) | async-done | bytes 5898272 | tf_op jit(solution)/shard_map/all_to_all | solution.py:346
  149.3 3.8 all-to-all-start.2
  153.1 1.3 dynamic_slice.34.orders_ref
  161.2 1.9 pad_maximum_fusion.fold_ref
  163.1 2.4 add_convert_fusion.unfold_ref
  165.5 103.4 %transform.2 = (bf16[32,9,5,16,128]{4,3,2,1,0:T(8,128)(2,1)}, f32[2560,128]{1,0:T(8,128)}, f32[1296,128]{1,0:T(8,128)}) custom-call(s32[20]{0:T(128)} %dynamic_slice.34.orders_ref, bf16[32,9,5,16,128]{4,3,2,1,0:T(8,128)(2,1)} %bitcast.1.arrived_ref, bf16[20,1281,640]{2,1,0:T(8,128)(2,1)} %legendre_ref.3, bf16[1280,1280]{1,0:T(8,128)(2,1)} %pad_maximum_fusion.fold_ref, ...), custom_call_target="tpu_custom_call" | custom-call | flops 31499999232 | bytes 27000000 | tf_op jit(solution)/shard_map/transform/pallas_call | solution.py:275
  269.0 44.4 %all-to-all-done.2 = bf16[32,880,128]{2,1,0:T(8,128)(2,1)} async-done(((bf16[32,880,128]{2,1,0:T(8,128)(2,1)}), bf16[32,880,128]{2,1,0:T(8,128)(2,1)}, u32[]{:S(2)}, u32[]{:S(2)}) %all-to-all-start.2) | async-done | bytes 7208992 | tf_op jit(solution)/shard_map/all_to_all | solution.py:346
  313.3 3.8 all-to-all-start.1
  317.1 125.4 %transform.3 = (bf16[32,11,5,16,128]{4,3,2,1,0:T(8,128)(2,1)}, f32[2560,128]{1,0:T(8,128)}, f32[1296,128]{1,0:T(8,128)}) custom-call(s32[20]{0:T(128)} %dynamic_slice.34.orders_ref, bf16[32,11,5,16,128]{4,3,2,1,0:T(8,128)(2,1)} %bitcast.11.arrived_ref, bf16[20,1281,640]{2,1,0:T(8,128)(2,1)} %legendre_ref.3, bf16[1280,1280]{1,0:T(8,128)(2,1)} %pad_maximum_fusion.fold_ref, ...), custom_call_target="tpu_custom_call" | custom-call | flops 38499999744 | bytes 33000000 | tf_op jit(solution)/shard_map/transform/pallas_call | solution.py:275
  442.5 5.8 all-to-all-done.1
  448.2 3.8 all-to-all-start.3
  452.1 1.3 add_add_fusion
  454.0 1.3 collective-permute-done
  455.6 1.6 collective-permute-start.1
  457.2 46.7 %collective-permute-done.1 = f32[8,20,128]{2,0,1:T(8,128)S(1)} collective-permute-done((f32[8,20,128]{2,0,1:T(8,128)S(1)}, f32[8,20,128]{2,0,1:T(8,128)S(1)}, u32[]{:S(2)}, u32[]{:S(2)}) %collective-permute-start.1) | collective-permute-done | bytes 81952 | tf_op jit(solution)/shard_map/ppermute | solution.py:338
  504.1 4.0 collective-permute-done.2
  508.2 2.1 collective-permute-start.3
  510.3 60.5 %collective-permute-done.3 = f32[2,20,128]{2,0,1:T(2,128)S(1)} collective-permute-done((f32[2,20,128]{2,0,1:T(2,128)S(1)}, f32[2,20,128]{2,0,1:T(2,128)S(1)}, u32[]{:S(2)}, u32[]{:S(2)}) %collective-permute-start.3) | collective-permute-done | bytes 20512 | tf_op jit(solution)/shard_map/ppermute | solution.py:338
  570.8 4.1 collective-permute-start.4
  574.9 37.7 %all-to-all-done.3 = bf16[32,880,128]{2,1,0:T(8,128)(2,1)} async-done(((bf16[32,880,128]{2,1,0:T(8,128)(2,1)}), bf16[32,880,128]{2,1,0:T(8,128)(2,1)}, u32[]{:S(2)}, u32[]{:S(2)}) %all-to-all-start.3) | async-done | bytes 7208992 | tf_op jit(solution)/shard_map/all_to_all | solution.py:346
  612.6 11.1 %scatter_waves.1 = bf16[40,1280,128]{2,1,0:T(8,128)(2,1)} custom-call(s32[640]{0:T(1024)} %table.5, bf16[32,9,5,16,128]{4,3,2,1,0:T(8,128)(2,1)} %bitcast.9.refs_0_, bf16[32,11,5,16,128]{4,3,2,1,0:T(8,128)(2,1)} %bitcast.13.refs_1_), custom_call_target="tpu_custom_call" | custom-call | bytes 26000000 | tf_op jit(solution)/shard_map/scatter_waves/pallas_call | solution.py:156
  (63 shorter events, 8.5 us)
Async XLA Ops:
  0.6 154.9 %copy-start = (f32[16,16]{1,0:T(8,128)S(1)}, f32[16,16]{1,0:T(8,128)}, u32[]{:S(2)}) copy-start(f32[16,16]{1,0:T(8,128)} %param.24) | copy-start | bytes 3076
  10.5 138.7 %all-to-all-start = ((bf16[32,720,128]{2,1,0:T(8,128)(2,1)}), bf16[32,720,128]{2,1,0:T(8,128)(2,1)}, u32[]{:S(2)}, u32[]{:S(2)}) async-start(bf16[32,720,128]{2,1,0:T(8,128)(2,1)} %bitcast.44), calls=%async_computation | async-start | bytes 11796480 | tf_op jit(solution)/shard_map/all_to_all | solution.py:346
  149.3 5.1 copy-start.7
  149.3 6.3 %copy-start.5 = (f32[16,16]{1,0:T(8,128)S(1)}, f32[16,16]{1,0:T(8,128)}, u32[]{:S(2)}) copy-start(f32[16,16]{1,0:T(8,128)} %param.25) | copy-start | bytes 3076
  149.3 7.2 %copy-start.9 = (f32[16]{0:T(128)S(1)}, f32[16]{0:T(128)}, u32[]{:S(2)}) copy-start(f32[16]{0:T(128)} %param.26) | copy-start | bytes 196
  149.3 7.9 %copy-start.8 = (f32[4,16]{1,0:T(4,128)S(1)}, f32[4,16]{1,0:T(4,128)}, u32[]{:S(2)}) copy-start(f32[4,16]{1,0:T(4,128)} %param.27) | copy-start | bytes 772
  149.3 10.1 %copy-start.6 = (s32[1280]{0:T(1024)S(1)}, s32[1280]{0:T(1024)}, u32[]{:S(2)}) copy-start(s32[1280]{0:T(1024)} %param.22) | copy-start | bytes 15364
  149.3 164.0 %all-to-all-start.2 = ((bf16[32,880,128]{2,1,0:T(8,128)(2,1)}), bf16[32,880,128]{2,1,0:T(8,128)(2,1)}, u32[]{:S(2)}, u32[]{:S(2)}) async-start(bf16[32,880,128]{2,1,0:T(8,128)(2,1)} %bitcast.43), calls=%async_computation.2 | async-start | bytes 14417920 | tf_op jit(solution)/shard_map/all_to_all | solution.py:346
  313.3 134.9 %all-to-all-start.1 = ((bf16[32,720,128]{2,1,0:T(8,128)(2,1)}), bf16[32,720,128]{2,1,0:T(8,128)(2,1)}, u32[]{:S(2)}, u32[]{:S(2)}) async-start(bf16[32,720,128]{2,1,0:T(8,128)(2,1)} %bitcast.46), calls=%async_computation.1 | async-start | bytes 11796480 | tf_op jit(solution)/shard_map/all_to_all | solution.py:346
  448.2 3.8 copy-start.2
  448.2 3.9 copy-start.3
  448.2 3.9 copy-start.4
  448.2 164.3 %all-to-all-start.3 = ((bf16[32,880,128]{2,1,0:T(8,128)(2,1)}), bf16[32,880,128]{2,1,0:T(8,128)(2,1)}, u32[]{:S(2)}, u32[]{:S(2)}) async-start(bf16[32,880,128]{2,1,0:T(8,128)(2,1)} %bitcast.45), calls=%async_computation.3 | async-start | bytes 14417920 | tf_op jit(solution)/shard_map/all_to_all | solution.py:346
  453.9 1.5 collective-permute-start
  455.6 48.4 %collective-permute-start.1 = (f32[8,20,128]{2,0,1:T(8,128)S(1)}, f32[8,20,128]{2,0,1:T(8,128)S(1)}, u32[]{:S(2)}, u32[]{:S(2)}) collective-permute-start(f32[8,20,128]{2,0,1:T(8,128)S(1)} %bitcast.57), channel_id=1, source_target_pairs={{0,2},{1,3},{2,0},{3,1},{4,6},{5,7},{6,4},{7,5},{8,10},{9,11},{10,... | collective-permute-start | bytes 245768 | tf_op jit(solution)/shard_map/ppermute | solution.py:338
  504.0 4.1 collective-permute-start.2
  508.2 62.6 %collective-permute-start.3 = (f32[2,20,128]{2,0,1:T(2,128)S(1)}, f32[2,20,128]{2,0,1:T(2,128)S(1)}, u32[]{:S(2)}, u32[]{:S(2)}) collective-permute-start(f32[2,20,128]{2,0,1:T(2,128)S(1)} %bitcast.62), channel_id=1, source_target_pairs={{0,8},{1,9},{2,10},{3,11},{4,12},{5,13},{6,14},{7,15},{8,0},{9,1},... | collective-permute-start | bytes 61448 | tf_op jit(solution)/shard_map/ppermute | solution.py:338
  570.8 52.9 %collective-permute-start.4 = (f32[1,20,128]{2,0,1:T(1,128)S(1)}, f32[1,20,128]{2,0,1:T(1,128)S(1)}, u32[]{:S(2)}, u32[]{:S(2)}) collective-permute-start(f32[1,20,128]{2,0,1:T(1,128)S(1)} %get-tuple-element.88), channel_id=1, source_target_pairs={{0,16},{1,17},{2,18},{3,19},{4,20},{5,21},{6,22},{7,23},{8,24},{9,... | collective-permute-start | bytes 30728 | tf_op jit(solution)/shard_map/ppermute | solution.py:338
  612.6 11.8 %copy-start.1 = (f32[16,16]{1,0:T(8,128)S(1)}, f32[16,16]{1,0:T(8,128)}, u32[]{:S(2)}) copy-start(f32[16,16]{1,0:T(8,128)} %param.24) | copy-start | bytes 3076
